TPU v7x, 512 devices: a whole 4x8x8 slice. The times are simulated.
512 devices in a mesh: fsdp: 64 (over y, z), store: 8 (over x, core).
Axes of the slice: x: 4, y: 8, z: 8, core: 2. Of those that a mesh axis runs over, the one named last changes fastest.
Arguments:
- layer_input: bfloat16 [16384, 5120], P('fsdp', 'store'), may hold values from -6 to 6
- gate_pre: bfloat16 [16384, 13824], P('fsdp', 'store'), may hold values from -6 to 6
- up_pre: bfloat16 [16384, 13824], P('fsdp', 'store'), may hold values from -6 to 6
- hidden_grad: bfloat16 [16384, 13824], P('fsdp', 'store'), may hold values from -6 to 6
- out_grad: bfloat16 [16384, 5120], P('fsdp', 'store'), may hold values from -6 to 6
- proj_model_in: bfloat16 [5120, 128], P('store'), may hold values from -0.078125 to 0.078125
- proj_hidden_in: bfloat16 [13824, 64], P('store'), may hold values from -0.0546875 to 0.0546875
- proj_hidden_out: bfloat16 [13824, 128], P('store'), may hold values from -0.0546875 to 0.0546875
- proj_model_out: bfloat16 [5120, 64], P('store'), may hold values from -0.078125 to 0.078125
- queries: bfloat16 [8192, 3, 4096], P('fsdp', None, 'store'), may hold values from -0.0546875 to 0.0546875
- validity: int32 [128, 128], P('fsdp'), may hold values 0 or 1
- owners: int32 [128], replicated, may hold values from 0 to 63, as said below
Outputs:
- scores: float32 [128, 8192], P('store', 'fsdp')
- stored: bfloat16 [256, 3, 4096], P('fsdp', None, 'store')
Inputs may be any that keep to these rules, and one draw needn't show every extreme that they name: `owners`: each owner owns at most 4 sequences, and some owner owns exactly 4.
All inputs are finite; a program needn't handle non-finite values. No bound on the sum of `validity` on one device may be relied on, other than what follows from the above.
Results may differ from a plain program's by a relative error of at most 0.0049.
Values may be sent and summed in bfloat16 or wider, within the bound.
No kernel may reach another device: no remote copies, remote signals or barrier semaphores. Data moves between devices by JAX's collectives and lax.ppermute only.
A program may use at most 64 MiB of HBM per device.

v0:
```python
import jax
import jax.numpy as jnp
from jax import lax
from jax.sharding import PartitionSpec as P


def local(
    layer_input,
    gate_pre,
    up_pre,
    hidden_grad,
    out_grad,
    proj_model_in,
    proj_hidden_in,
    proj_hidden_out,
    proj_model_out,
    queries,
    validity,
    owners,
):
    factor_width = proj_hidden_in.shape[1]
    seq_count, seq_len = validity.shape
    gate32 = gate_pre.astype(jnp.float32)
    up32 = up_pre.astype(jnp.float32)
    dh32 = hidden_grad.astype(jnp.float32)
    sigma = jax.nn.sigmoid(gate32)
    hidden = (gate32 * sigma * up32).astype(jnp.bfloat16)
    gate_grad = (dh32 * up32 * sigma * (1.0 + gate32 * (1.0 - sigma))).astype(jnp.bfloat16)
    up_grad = (dh32 * (gate32 * sigma)).astype(jnp.bfloat16)
    from_model = jnp.dot(layer_input, proj_model_in, preferred_element_type=jnp.float32)
    in_part = jnp.stack(
        [
            from_model[:, :factor_width],
            from_model[:, factor_width:],
            jnp.dot(hidden, proj_hidden_in, preferred_element_type=jnp.float32),
        ],
        axis=1,
    )
    out_part = jnp.stack(
        [
            jnp.dot(
                gate_grad, proj_hidden_out[:, :factor_width], preferred_element_type=jnp.float32
            ),
            jnp.dot(up_grad, proj_hidden_out[:, factor_width:], preferred_element_type=jnp.float32),
            jnp.dot(out_grad, proj_model_out, preferred_element_type=jnp.float32),
        ],
        axis=1,
    )
    weights = validity.astype(jnp.float32)
    in_full = lax.psum(in_part, "store")
    out_rows = lax.psum_scatter(out_part, "store", scatter_dimension=2, tiled=True)
    summed = jnp.einsum(
        "el,elmi,elmj->emij",
        weights,
        out_rows.reshape(seq_count, seq_len, 3, -1),
        in_full.reshape(seq_count, seq_len, 3, factor_width),
        precision=lax.Precision.HIGHEST,
    )
    sketch_local = (
        (summed * float(seq_len) ** (-0.5)).reshape(seq_count, 3, -1).astype(jnp.bfloat16)
    )
    query_rows = queries.reshape(queries.shape[0], -1)
    capacity = 2 * seq_count
    own_index = lax.axis_index("fsdp")
    is_mine = (owners == own_index).astype(jnp.int32)
    slot_rank = jnp.cumsum(is_mine) - is_mine
    chooser = (
        (slot_rank[None, :] == jnp.arange(capacity, dtype=jnp.int32)[:, None])
        & (is_mine[None, :] == 1)
    ).astype(jnp.bfloat16)
    piece = lax.all_gather(sketch_local, "fsdp", axis=0, tiled=True)
    row_count = piece.shape[0]
    flattened = piece.reshape(row_count, -1)
    block = lax.dot_general(
        flattened, query_rows, (((1,), (1,)), ((), ())), preferred_element_type=jnp.float32
    )
    partial_scores = block
    kept = jnp.dot(chooser, flattened, preferred_element_type=jnp.float32)
    kept, partial_scores = (kept, partial_scores)
    scores = lax.psum_scatter(partial_scores, "store", scatter_dimension=0, tiled=True)
    stored = kept.reshape(capacity, 3, -1).astype(jnp.bfloat16)
    return (scores, stored)


def solution(mesh):
    placed = (
        P("fsdp", "store"),
        P("fsdp", "store"),
        P("fsdp", "store"),
        P("fsdp", "store"),
        P("fsdp", "store"),
        P("store", None),
        P("store", None),
        P("store", None),
        P("store", None),
        P("fsdp", None, "store"),
        P("fsdp", None),
        P(),
    )
    return jax.shard_map(
        local,
        mesh=mesh,
        in_specs=placed,
        out_specs=(P("store", "fsdp"), P("fsdp", None, "store")),
        check_vma=False,
    )
```

profile of v0, /device:TPU:1, one launch (start us, length us, event | category | flops | bytes accessed | tf_op | source)
XLA Modules:
  0.0 214.7 jit_solution(4459848732300982850)
XLA Ops:
  7.2 0.0 copy-start
  7.2 0.0 copy-start.9
  7.2 0.0 all-reduce.2.cloned.1.call-start
  7.2 1.4 fusion.27
  8.6 0.0 copy-done.9
  8.7 0.0 copy-start.6
  8.7 0.0 copy-start.7
  8.7 0.0 copy-start.8
  8.7 2.2 %convolution_bitcast_fusion.2 = f32[256,1,64]{0,2,1:T(8,128)S(1)} fusion(bf16[1728,64]{0,1:T(8,128)(2,1)S(1)} %copy-done.9, bf16[256,1728]{0,1:T(8,128)(2,1)} %param.14, bf16[256,1728]{0,1:T(8,128)(2,1)} %param.13), kind=kOutput, calls=%fused_computation.17 | convolution fusion | flops 60162048 | bytes 2056192 | tf_op jit(solution)/shard_map/dot_general | solution.py:35
  10.9 0.7 copy_bitcast_fusion
  11.6 0.0 all-reduce.2.cloned.1.call-update
  11.7 0.0 copy-start.5
  11.7 0.0 reduce-scatter.3.cloned.1.call-start
  11.7 0.0 copy-done.6
  11.7 0.0 copy-done.7
  11.8 0.0 copy-done.8
  11.8 0.8 convolution_bitcast_fusion
  12.6 0.3 copy-done.5
  12.8 0.0 copy-start.1
  12.8 0.0 copy-start.2
  12.8 1.0 convolution_bitcast_fusion.1
  13.8 0.0 copy-done.1
  13.8 0.0 copy-done.2
  13.8 0.0 copy-start.4
  13.8 0.0 copy-start.3
  13.9 0.2 convolution_bitcast_fusion.4
  14.1 0.7 pad_maximum_fusion
  14.8 0.0 reduce-scatter.3.cloned.1.call-update
  14.8 0.0 reduce-scatter.5.cloned.1.call-start
  14.9 0.0 copy-done.4
  14.9 0.0 copy-done.3
  14.9 0.1 copy.28
  15.0 0.2 reduce-window.9
  15.2 0.1 reduce
  15.3 70.9 %all-reduce.2.cloned.1.call-done = f32[2,128,3,64]{1,3,2,0:T(8,128)} async-done(((f32[2,128,3,64]{1,3,2,0:T(8,128)}), f32[2,128,3,64]{1,3,2,0:T(8,128)}) %all-reduce.2.cloned.1.call-update) | async-done | bytes 196624 | tf_op jit(solution)/shard_map/psum | solution.py:50
  86.2 37.8 %reduce-scatter.3.cloned.1.call-done = f32[256,3,8]{0,2,1:T(8,128)} async-done(((f32[256,3,64]{0,2,1:T(8,128)}), f32[256,3,8]{0,2,1:T(8,128)}) %reduce-scatter.3.cloned.1.call-update) | async-done | bytes 24592 | tf_op jit(solution)/shard_map/reduce_scatter | solution.py:51
  124.0 1.4 fusion.9
  125.4 0.1 reshape.54
  125.5 38.4 %all_gather.3 = bf16[128,3,512]{2,1,0:T(4,128)(2,1)S(1)} all-gather(bf16[2,3,512]{2,1,0:T(4,128)(2,1)S(1)} %reshape.54), channel_id=1, replica_groups=mesh['fsdp'=64,'store'=8] {'fsdp'}, dimensions={0}, use_global_device_ids=true | all-gather | bytes 399360 | tf_op jit(solution)/shard_map/all_gather | solution.py:71
  163.9 0.3 copy.29
  164.2 0.0 copy-done
  164.2 0.9 convolution_bitcast_fusion.3
  165.2 0.0 reduce-scatter.5.cloned.1.call-update
  165.2 0.8 convolution_convert_fusion
  166.0 42.1 %reduce-scatter.5.cloned.1.call-done = f32[16,128]{1,0:T(8,128)} async-done(((f32[128,128]{1,0:T(8,128)}), f32[16,128]{1,0:T(8,128)}) %reduce-scatter.5.cloned.1.call-update) | async-done | bytes 8208 | tf_op jit(solution)/shard_map/reduce_scatter | solution.py:80
  (4 shorter events, 0.0 us)
Async XLA Ops:
  7.2 157.1 %copy-start = (bf16[128,3,512]{2,0,1:T(8,128)(2,1)S(1)}, bf16[128,3,512]{2,0,1:T(8,128)(2,1)}, u32[]{:S(2)}) copy-start(bf16[128,3,512]{2,0,1:T(8,128)(2,1)} %param.21) | copy-start | bytes 1179652
  7.2 1.5 copy-start.9
  7.2 79.1 %all-reduce.2.cloned.1.call-start = ((), (), s32[]{:S(2)}) async-start(), calls=%async_computation.3 | async-start | bytes 393216 | tf_op jit(solution)/shard_map/psum | solution.py:50
  8.7 3.1 %copy-start.6 = (bf16[256,1728]{0,1:T(8,128)(2,1)S(1)}, bf16[256,1728]{0,1:T(8,128)(2,1)}, u32[]{:S(2)}) copy-start(bf16[256,1728]{0,1:T(8,128)(2,1)} %param.13) | copy-start | bytes 2654212
  8.7 3.1 %copy-start.7 = (bf16[256,1728]{0,1:T(8,128)(2,1)S(1)}, bf16[256,1728]{0,1:T(8,128)(2,1)}, u32[]{:S(2)}) copy-start(bf16[256,1728]{0,1:T(8,128)(2,1)} %param.15) | copy-start | bytes 2654212
  8.7 3.1 %copy-start.8 = (bf16[1728,128]{1,0:T(8,128)(2,1)S(1)}, bf16[1728,128]{1,0:T(8,128)(2,1)}, u32[]{:S(2)}) copy-start(bf16[1728,128]{1,0:T(8,128)(2,1)} %param.19) | copy-start | bytes 1327108
  11.7 1.2 copy-start.5
  11.7 112.4 %reduce-scatter.3.cloned.1.call-start = ((), (), s32[]{:S(2)}) async-start(), calls=%async_computation.2 | async-start | bytes 221184 | tf_op jit(solution)/shard_map/reduce_scatter | solution.py:51
  12.8 1.0 copy-start.1
  12.8 1.0 copy-start.2
  13.8 1.0 copy-start.4
  13.8 1.1 copy-start.3
  14.8 193.3 %reduce-scatter.5.cloned.1.call-start = ((), (), s32[]{:S(2)}) async-start(), calls=%async_computation.4 | async-start | bytes 73728 | tf_op jit(solution)/shard_map/reduce_scatter | solution.py:80
Sparse Core Ops, SparseCore 0:
  11.8 74.4 all-reduce.1
  89.3 34.7 reduce-scatter.2
  165.3 42.8 reduce-scatter.4
where the time goes:
time: 215 us
  waiting for transfers between devices  151 us (70%)
  blocking collectives  38.4 us (18%)
  between operations  13.9 us (6%)
  matrix products  8.67 us (4%)
    psum x1, waiting for transfers between devices, local(): in_full = lax.psum(in_part, 'store')  70.9 us
    reduce_scatter x1, waiting for transfers between devices, local(): lax.psum_scatter(partial_scores, 'store', scatter_dimension=0, tiled=True)  42.1 us
    all_gather x1, blocking collectives, local(): piece = lax.all_gather(sketch_local, 'fsdp', axis=0, tiled=True)  38.4 us
    reduce_scatter x1, waiting for transfers between devices, local(): lax.psum_scatter(out_part, 'store', scatter_dimension=2, tiled=True)  37.8 us
  transfers between devices with their start and end apart: 3, of which 3 were waited for; matrix products, arithmetic and copies ran while one was open for 2% of the time, Pallas kernels for 0%

commit v1 on v0

v1 whole, which is shorter than its diff:
```python
import jax
import jax.numpy as jnp
from jax import lax
from jax.sharding import PartitionSpec as P


def local(
    layer_input,
    gate_pre,
    up_pre,
    hidden_grad,
    out_grad,
    proj_model_in,
    proj_hidden_in,
    proj_hidden_out,
    proj_model_out,
    queries,
    validity,
    owners,
):
    rank = proj_hidden_in.shape[1]
    seq_count, seq_len = validity.shape
    stores = lax.axis_size("store")
    groups = lax.axis_size("fsdp")
    rows = rank // stores
    gate32 = gate_pre.astype(jnp.float32)
    up32 = up_pre.astype(jnp.float32)
    dh32 = hidden_grad.astype(jnp.float32)
    sigma = jax.nn.sigmoid(gate32)
    hidden = (gate32 * sigma * up32).astype(jnp.bfloat16)
    gate_grad = (dh32 * up32 * sigma * (1.0 + gate32 * (1.0 - sigma))).astype(jnp.bfloat16)
    up_grad = (dh32 * (gate32 * sigma)).astype(jnp.bfloat16)

    def factor(proj, act):
        return lax.dot_general(
            proj, act, (((0,), (1,)), ((), ())), preferred_element_type=jnp.float32
        ).astype(jnp.bfloat16)

    tokens = gate_pre.shape[0]
    in_part = jnp.concatenate(
        [factor(proj_model_in, layer_input), factor(proj_hidden_in, hidden)], axis=0
    )
    out_part = jnp.concatenate(
        [
            factor(proj_hidden_out[:, :rank], gate_grad),
            factor(proj_hidden_out[:, rank:], up_grad),
            factor(proj_model_out, out_grad),
        ],
        axis=0,
    )
    out_blocks = out_part.reshape(3, stores, rows, tokens).transpose(1, 0, 2, 3)
    send = jnp.concatenate(
        [
            jnp.broadcast_to(in_part[None], (stores, 3 * rank, tokens)),
            out_blocks.reshape(stores, 3 * rows, tokens),
        ],
        axis=1,
    )
    got = lax.all_to_all(send, "store", 0, 0, tiled=True)
    full = jnp.sum(got.astype(jnp.float32), axis=0)
    in_full = full[: 3 * rank].reshape(3, rank, seq_count, seq_len)
    out_rows = full[3 * rank :].reshape(3, rows, seq_count, seq_len)
    weights = validity.astype(jnp.float32)
    summed = jnp.einsum(
        "mjel,miel->emij",
        in_full,
        out_rows * weights,
        precision=lax.Precision.HIGHEST,
    )
    sketch_local = (summed * float(seq_len) ** (-0.5)).astype(jnp.bfloat16)
    flat_local = sketch_local.reshape(1, seq_count, 3 * rows * rank)
    spread = jnp.broadcast_to(flat_local, (groups, seq_count, 3 * rows * rank))
    gathered = lax.all_to_all(spread, "fsdp", 0, 0, tiled=True)
    flattened = gathered.reshape(groups * seq_count, 3 * rows * rank)
    query_rows = queries.reshape(queries.shape[0], -1)
    partial_scores = lax.dot_general(
        flattened, query_rows, (((1,), (1,)), ((), ())), preferred_element_type=jnp.float32
    )
    capacity = 2 * seq_count
    own_index = lax.axis_index("fsdp")
    is_mine = (owners == own_index).astype(jnp.int32)
    count = owners.shape[0]
    before = lax.broadcasted_iota(jnp.int32, (count, count), 0) < lax.broadcasted_iota(
        jnp.int32, (count, count), 1
    )
    slot_rank = jnp.sum(jnp.where(before, is_mine[:, None], 0), axis=0)
    chooser = (
        (slot_rank[None, :] == jnp.arange(capacity, dtype=jnp.int32)[:, None])
        & (is_mine[None, :] == 1)
    ).astype(jnp.bfloat16)
    kept = jnp.dot(chooser, flattened, preferred_element_type=jnp.float32)
    stored = kept.reshape(capacity, 3, -1).astype(jnp.bfloat16)
    score_blocks = lax.all_to_all(
        partial_scores.reshape(stores, -1, partial_scores.shape[1]), "store", 0, 0, tiled=True
    )
    scores = jnp.sum(score_blocks, axis=0)
    return (scores, stored)


def solution(mesh):
    placed = (
        P("fsdp", "store"),
        P("fsdp", "store"),
        P("fsdp", "store"),
        P("fsdp", "store"),
        P("fsdp", "store"),
        P("store", None),
        P("store", None),
        P("store", None),
        P("store", None),
        P("fsdp", None, "store"),
        P("fsdp", None),
        P(),
    )
    return jax.shard_map(
        local,
        mesh=mesh,
        in_specs=placed,
        out_specs=(P("store", "fsdp"), P("fsdp", None, "store")),
        check_vma=False,
    )
```

time: 215 us -> 73.3 us (0.34)
  waiting for transfers between devices: 151 us -> 31.4 us
  blocking collectives: 38.4 us -> 0 us
  starting transfers between devices: 0.12 us -> 29.1 us
  between operations: 13.9 us -> 0.89 us
    reduce_scatter x2 -> x0, waiting for transfers between devices: 80 us -> none  [the longest x1 42.1 us: local(): lax.psum_scatter(partial_scores, 'store', scatter_dimension=0, tiled=True)]
    psum x1 -> x0, waiting for transfers between devices: 70.9 us -> none  [local(): in_full = lax.psum(in_part, 'store')]
    all_gather x1 -> x0, blocking collectives: 38.4 us -> none  [local(): piece = lax.all_gather(sketch_local, 'fsdp', axis=0, tiled=True)]
    all_to_all x0 -> x3, waiting for transfers between devices: none -> 31.4 us  [the longest x1 14 us: local(): gathered = lax.all_to_all(spread, 'fsdp', 0, 0, tiled=True)]
    all_to_all x0 -> x3, starting transfers between devices: none -> 29.1 us  [the longest x1 11.9 us: local(): gathered = lax.all_to_all(spread, 'fsdp', 0, 0, tiled=True)]
where the time goes in v1:
time: 73.3 us; the launch traced here: 73 us
  waiting for transfers between devices  31.4 us (43%)
  starting transfers between devices  29.1 us (40%)
  matrix products  6.67 us (9%)
  local copies, waits for them, and re-layouts  3 us (4%)
  other arithmetic  1.86 us (3%)
  between operations  0.89 us (1%)
    all_to_all x1, waiting for transfers between devices, local(): gathered = lax.all_to_all(spread, 'fsdp', 0, 0, tiled=True)  14 us
    all_to_all x1, waiting for transfers between devices, local(): got = lax.all_to_all(send, 'store', 0, 0, tiled=True)  13.4 us
    all_to_all x1, starting transfers between devices, local(): gathered = lax.all_to_all(spread, 'fsdp', 0, 0, tiled=True)  11.9 us
    all_to_all x1, starting transfers between devices, local(): got = lax.all_to_all(send, 'store', 0, 0, tiled=True)  10.5 us
    all_to_all x1, starting transfers between devices, local(): lax.all_to_all(partial_scores.reshape(stores, -1, partial_scores.shape[1]...  6.77 us
    dot_general x5, matrix products, factor(): lax.dot_general(proj, act, (((0,), (1,)), ((), ())), preferred_element_ty...  4.56 us
    all_to_all x1, waiting for transfers between devices, local(): lax.all_to_all(partial_scores.reshape(stores, -1, partial_scores.shape[1]...  4.05 us
  transfers between devices with their start and end apart: 3, of which 3 were waited for; matrix products, arithmetic and copies ran while one was open for 2% of the time, Pallas kernels for 0%

profile of v1, /device:TPU:1, one launch (start us, length us, event | category | flops | bytes accessed | tf_op | source)
XLA Modules:
  0.0 73.0 jit_solution(14167245171554354142)
XLA Ops:
  0.6 0.0 copy-start
  0.6 0.0 copy-start.8
  0.7 0.0 copy-start.7
  0.7 0.0 copy-start.10
  0.7 0.0 copy-start.9
  0.7 2.5 %fusion.10 = bf16[64,256]{1,0:T(8,128)(2,1)S(1)} fusion(bf16[256,1728]{0,1:T(8,128)(2,1)} %param.15, bf16[256,1728]{0,1:T(8,128)(2,1)} %param.13, bf16[1728,128]{1,0:T(8,128)(2,1)} %param.19), kind=kOutput, calls=%fused_computation.22 | convolution fusion | flops 60178432 | bytes 2244608 | tf_op jit(solution)/shard_map/dot_general | solution.py:35
  3.2 0.0 copy-done.8
  3.2 0.0 copy-done.7
  3.2 0.0 copy-done.10
  3.2 0.0 copy-done.9
  3.2 0.0 copy-start.11
  3.2 1.0 %fusion.9 = bf16[64,256]{1,0:T(8,128)(2,1)S(1)} fusion(bf16[256,1728]{0,1:T(8,128)(2,1)S(1)} %copy-done.9, bf16[256,1728]{0,1:T(8,128)(2,1)S(1)} %copy-done.7, bf16[256,1728]{0,1:T(8,128)(2,1)S(1)} %copy-done.8, bf16[1728,128]{1,0:T(8,128)(2,1)S(1)} %copy-done.10), kind=kOutput, calls=%fused_computation.21 | convolution fusion | flops 62390272 | bytes 3129344 | tf_op jit(solution)/shard_map/dot_general | solution.py:35
  4.2 0.0 copy-done.11
  4.2 0.0 copy-start.2
  4.2 0.0 copy-start.4
  4.2 0.6 fusion.11
  4.9 0.3 copy-done.2
  5.2 0.0 copy-done.4
  5.2 0.0 copy-start.3
  5.2 0.2 convolution_convert_fusion.4
  5.5 0.0 copy-done
  5.5 0.6 copy-done.3
  6.1 0.3 convolution_convert_fusion
  6.4 0.1 broadcast_in_dim.18
  6.5 1.0 %pad_maximum_fusion = bf16[8,216,256]{2,1,0:T(8,128)(2,1)} fusion(bf16[8,24,256]{2,1,0:T(8,128)(2,1)S(1)} %bitcast.39, bf16[8,192,256]{2,1,0:T(8,128)(2,1)S(1)} %broadcast_in_dim.18), kind=kLoop, calls=%fused_computation.27 | loop fusion | flops 1769472 | bytes 1769472 | tf_op jit(solution)/shard_map/concatenate | solution.py:52
  7.5 10.5 %all-to-all-start = ((bf16[8,216,256]{2,1,0:T(8,128)(2,1)}), bf16[8,216,256]{2,1,0:T(8,128)(2,1)S(1)}, u32[]{:S(2)}, u32[]{:S(2)}) async-start(bf16[8,216,256]{2,1,0:T(8,128)(2,1)} %pad_maximum_fusion), calls=%async_computation | async-start | bytes 1769472 | tf_op jit(solution)/shard_map/all_to_all | solution.py:59
  17.9 0.0 copy-done.5
  17.9 13.4 %all-to-all-done = bf16[8,216,256]{2,1,0:T(8,128)(2,1)S(1)} async-done(((bf16[8,216,256]{2,1,0:T(8,128)(2,1)}), bf16[8,216,256]{2,1,0:T(8,128)(2,1)S(1)}, u32[]{:S(2)}, u32[]{:S(2)}) %all-to-all-start) | async-done | bytes 884768 | tf_op jit(solution)/shard_map/all_to_all | solution.py:59
  31.3 0.1 convert_reduce_fusion
  31.4 0.0 copy-start.1
  31.4 0.1 reshape.38
  31.6 0.4 fusion.12
  32.0 0.1 broadcast_in_dim.19
  32.1 1.0 %broadcast_in_dim.32 = bf16[64,2,1536]{2,1,0:T(2,128)(2,1)} broadcast(bf16[2,1536]{1,0:T(2,128)(2,1)S(1)} %broadcast_in_dim.19), dimensions={1,2} | broadcast | bytes 399360 | tf_op jit(solution)/shard_map/broadcast_in_dim | solution.py:72
  33.0 11.9 %all-to-all-start.1 = ((bf16[64,2,1536]{2,1,0:T(2,128)(2,1)}), bf16[64,2,1536]{2,1,0:T(2,128)(2,1)S(1)}, u32[]{:S(2)}, u32[]{:S(2)}) async-start(bf16[64,2,1536]{2,1,0:T(2,128)(2,1)} %broadcast_in_dim.32), calls=%async_computation.1 | async-start | bytes 786432 | tf_op jit(solution)/shard_map/all_to_all | solution.py:73
  44.9 0.0 copy-done.1
  44.9 0.2 copy.24
  45.2 0.0 copy-done.6
  45.2 0.1 select_reduce_fusion
  45.3 14.0 %all-to-all-done.1 = bf16[64,2,1536]{2,1,0:T(2,128)(2,1)S(1)} async-done(((bf16[64,2,1536]{2,1,0:T(2,128)(2,1)}), bf16[64,2,1536]{2,1,0:T(2,128)(2,1)S(1)}, u32[]{:S(2)}, u32[]{:S(2)}) %all-to-all-start.1) | async-done | bytes 393248 | tf_op jit(solution)/shard_map/all_to_all | solution.py:73
  59.3 0.1 reshape.40
  59.5 0.2 copy.26
  59.7 0.1 dot_general.36
  59.8 0.9 %fusion.29 = f32[8,16,128]{2,1,0:T(8,128)} fusion(bf16[8,16,1536]{2,1,0:T(8,128)(2,1)S(1)} %dot_general.36, bf16[128,1536,1]{0,1,2:T(8,128)(2,1)S(1)} %bitcast.38), kind=kOutput, calls=%fused_computation.49 | convolution fusion | flops 50331648 | bytes 851968 | tf_op jit(solution)/shard_map/dot_general | solution.py:76
  60.7 6.8 %all-to-all-start.2 = ((f32[8,16,128]{2,1,0:T(8,128)}), f32[8,16,128]{2,1,0:T(8,128)S(1)}, u32[]{:S(2)}, u32[]{:S(2)}) async-start(f32[8,16,128]{2,1,0:T(8,128)} %fusion.29), calls=%async_computation.2 | async-start | bytes 131072 | tf_op jit(solution)/shard_map/all_to_all | solution.py:93
  67.5 0.8 %convolution_convert_fusion.5 = bf16[4,3,512]{2,0,1:T(4,128)(2,1)} fusion(bf16[3,512,128]{2,1,0:T(8,128)(2,1)S(1)} %bitcast.37, s32[128]{0:T(128)S(1)} %select_reduce_fusion, pred[128]{0:T(512)(128)(4,1)S(1)} %get-tuple-element.2), kind=kOutput, calls=%fused_computation.26 | convolution fusion | flops 1580032 | bytes 406144 | tf_op jit(solution)/shard_map/dot_general | solution.py:91
  68.3 4.1 %all-to-all-done.2 = f32[8,16,128]{2,1,0:T(8,128)S(1)} async-done(((f32[8,16,128]{2,1,0:T(8,128)}), f32[8,16,128]{2,1,0:T(8,128)S(1)}, u32[]{:S(2)}, u32[]{:S(2)}) %all-to-all-start.2) | async-done | bytes 65568 | tf_op jit(solution)/shard_map/all_to_all | solution.py:93
  72.4 0.6 reduce_sum.28
  (8 shorter events, 0.1 us)
Async XLA Ops:
  0.6 4.8 %copy-start = (bf16[256,640]{1,0:T(8,128)(2,1)S(1)}, bf16[256,640]{1,0:T(8,128)(2,1)}, u32[]{:S(2)}) copy-start(bf16[256,640]{1,0:T(8,128)(2,1)} %param.12) | copy-start | bytes 983044
  0.6 2.5 %copy-start.8 = (bf16[256,1728]{0,1:T(8,128)(2,1)S(1)}, bf16[256,1728]{0,1:T(8,128)(2,1)}, u32[]{:S(2)}) copy-start(bf16[256,1728]{0,1:T(8,128)(2,1)} %param.13) | copy-start | bytes 2654212
  0.7 2.5 %copy-start.7 = (bf16[256,1728]{0,1:T(8,128)(2,1)S(1)}, bf16[256,1728]{0,1:T(8,128)(2,1)}, u32[]{:S(2)}) copy-start(bf16[256,1728]{0,1:T(8,128)(2,1)} %param.15) | copy-start | bytes 2654212
  0.7 2.5 %copy-start.10 = (bf16[1728,128]{1,0:T(8,128)(2,1)S(1)}, bf16[1728,128]{1,0:T(8,128)(2,1)}, u32[]{:S(2)}) copy-start(bf16[1728,128]{1,0:T(8,128)(2,1)} %param.19) | copy-start | bytes 1327108
  0.7 2.5 %copy-start.9 = (bf16[256,1728]{0,1:T(8,128)(2,1)S(1)}, bf16[256,1728]{0,1:T(8,128)(2,1)}, u32[]{:S(2)}) copy-start(bf16[256,1728]{0,1:T(8,128)(2,1)} %param.14) | copy-start | bytes 2654212
  3.2 1.0 %copy-start.11 = (bf16[1728,64]{0,1:T(8,128)(2,1)S(1)}, bf16[1728,64]{0,1:T(8,128)(2,1)}, u32[]{:S(2)}) copy-start(bf16[1728,64]{0,1:T(8,128)(2,1)} %param.18) | copy-start | bytes 663556
  4.2 1.0 %copy-start.2 = (bf16[256,640]{1,0:T(8,128)(2,1)S(1)}, bf16[256,640]{1,0:T(8,128)(2,1)}, u32[]{:S(2)}) copy-start(bf16[256,640]{1,0:T(8,128)(2,1)} %param.16) | copy-start | bytes 983044
  4.2 1.0 %copy-start.4 = (bf16[640,64]{0,1:T(8,128)(2,1)S(1)}, bf16[640,64]{0,1:T(8,128)(2,1)}, u32[]{:S(2)}) copy-start(bf16[640,64]{0,1:T(8,128)(2,1)} %param.20) | copy-start | bytes 245764
  5.2 0.9 %copy-start.3 = (bf16[640,128]{1,0:T(8,128)(2,1)S(1)}, bf16[640,128]{1,0:T(8,128)(2,1)}, u32[]{:S(2)}) copy-start(bf16[640,128]{1,0:T(8,128)(2,1)} %param.17) | copy-start | bytes 491524
  7.5 10.5 %copy-start.5 = (s32[2,128]{1,0:T(2,128)S(1)}, s32[2,128]{1,0:T(2,128)}, u32[]{:S(2)}) copy-start(s32[2,128]{1,0:T(2,128)} %param.22) | copy-start | bytes 3076
  7.5 23.8 %all-to-all-start = ((bf16[8,216,256]{2,1,0:T(8,128)(2,1)}), bf16[8,216,256]{2,1,0:T(8,128)(2,1)S(1)}, u32[]{:S(2)}, u32[]{:S(2)}) async-start(bf16[8,216,256]{2,1,0:T(8,128)(2,1)} %pad_maximum_fusion), calls=%async_computation | async-start | bytes 1769472 | tf_op jit(solution)/shard_map/all_to_all | solution.py:59
  31.4 13.5 %copy-start.1 = (bf16[128,3,512]{2,0,1:T(8,128)(2,1)S(1)}, bf16[128,3,512]{2,0,1:T(8,128)(2,1)}, u32[]{:S(2)}) copy-start(bf16[128,3,512]{2,0,1:T(8,128)(2,1)} %param.21) | copy-start | bytes 1179652
  33.0 12.1 %copy-start.6 = (s32[128]{0:T(128)S(1)}, s32[128]{0:T(128)}, u32[]{:S(2)}) copy-start(s32[128]{0:T(128)} %param.23) | copy-start | bytes 1540
  33.0 26.3 %all-to-all-start.1 = ((bf16[64,2,1536]{2,1,0:T(2,128)(2,1)}), bf16[64,2,1536]{2,1,0:T(2,128)(2,1)S(1)}, u32[]{:S(2)}, u32[]{:S(2)}) async-start(bf16[64,2,1536]{2,1,0:T(2,128)(2,1)} %broadcast_in_dim.32), calls=%async_computation.1 | async-start | bytes 786432 | tf_op jit(solution)/shard_map/all_to_all | solution.py:73
  60.7 11.6 %all-to-all-start.2 = ((f32[8,16,128]{2,1,0:T(8,128)}), f32[8,16,128]{2,1,0:T(8,128)S(1)}, u32[]{:S(2)}, u32[]{:S(2)}) async-start(f32[8,16,128]{2,1,0:T(8,128)} %fusion.29), calls=%async_computation.2 | async-start | bytes 131072 | tf_op jit(solution)/shard_map/all_to_all | solution.py:93

commit v2 on v0

v2 whole, which is shorter than its diff:
```python
import functools

import jax
import jax.numpy as jnp
from jax import lax
from jax.experimental import pallas as pl
from jax.experimental.pallas import tpu as pltpu
from jax.sharding import PartitionSpec as P

BF = jnp.bfloat16
F32 = jnp.float32


def _dot(a, b, ca, cb, **kw):
    return lax.dot_general(
        a, b, (((ca,), (cb,)), ((), ())), preferred_element_type=F32, **kw
    )


def _splits(total, step):
    return [(lo, min(lo + step, total)) for lo in range(0, total, step)]


def factor_kernel(
    stores,
    step,
    x_hbm,
    gate_hbm,
    up_hbm,
    dh_hbm,
    dy_hbm,
    pmi_hbm,
    phi_hbm,
    pho_hbm,
    pmo_hbm,
    out_ref,
    x,
    gate,
    up,
    dh,
    dy,
    pmi,
    phi,
    pho,
    pmo,
    hidden,
    gate_grad,
    up_grad,
    sems,
):
    features, tokens = gate.shape
    rank = phi.shape[0]
    rows = rank // stores
    seq_len = out_ref.shape[2]
    spans = _splits(features, step)
    model = [
        pltpu.make_async_copy(src, dst, sems.at[i])
        for i, (src, dst) in enumerate(
            [(x_hbm, x), (pmi_hbm, pmi), (dy_hbm, dy), (pmo_hbm, pmo), (phi_hbm, phi), (pho_hbm, pho)]
        )
    ]
    parts = [
        [
            pltpu.make_async_copy(
                src.at[pl.ds(lo, hi - lo)], dst.at[pl.ds(lo, hi - lo)], sems.at[6 + 3 * n + i]
            )
            for i, (src, dst) in enumerate([(gate_hbm, gate), (up_hbm, up), (dh_hbm, dh)])
        ]
        for n, (lo, hi) in enumerate(spans)
    ]
    for copy in model + parts[0]:
        copy.start()
    for part in parts[1:]:
        for copy in part:
            copy.start()

    for copy in model[:4]:
        copy.wait()
    from_model = _dot(x[...], pmi[...], 1, 0).T
    out_two = _dot(pmo[...], dy[...], 1, 1)
    for copy in model[4:]:
        copy.wait()
    in_two = out_zero = out_one = None
    for n, (lo, hi) in enumerate(spans):
        for copy in parts[n]:
            copy.wait()
        block = 64

        def body(i, carry, lo=lo):
            at = pl.ds(pl.multiple_of(lo + i * block, block), block)
            g = gate[at].astype(F32)
            u = up[at].astype(F32)
            d = dh[at].astype(F32)
            sigma = 0.5 * jnp.tanh(0.5 * g) + 0.5
            silu = g * sigma
            hidden[at] = (silu * u).astype(BF)
            up_grad[at] = (d * silu).astype(BF)
            gate_grad[at] = (d * u * (sigma + silu * (1.0 - sigma))).astype(BF)
            return carry

        lax.fori_loop(0, (hi - lo) // block, body, 0, unroll=True)
        a = _dot(phi[:, lo:hi], hidden[lo:hi], 1, 0)
        b = _dot(pho[lo:hi, :rank], gate_grad[lo:hi], 0, 0)
        c = _dot(pho[lo:hi, rank:], up_grad[lo:hi], 0, 0)
        in_two = a if in_two is None else in_two + a
        out_zero = b if out_zero is None else out_zero + b
        out_one = c if out_one is None else out_one + c

    out_all = [out_zero, out_one, out_two]
    for e in range(2):
        at = slice(e * seq_len, (e + 1) * seq_len)
        factors = jnp.concatenate([from_model[:, at], in_two[:, at]], axis=0).astype(BF)
        for s in range(e, stores, 2):
            out_ref[s, : 3 * rank] = factors
            for m in range(3):
                mine = out_all[m][s * rows : (s + 1) * rows, at]
                other = out_all[m][(s ^ 1) * rows : ((s ^ 1) + 1) * rows, at]
                lo = 3 * rank + m * 2 * rows
                out_ref[s, lo : lo + 2 * rows] = jnp.concatenate([mine, other], axis=0).astype(BF)


def sketch_kernel(scale, got, weights, out_ref, total):
    stores = got.shape[0]
    acc = got[0].astype(F32)
    for s in range(1, stores):
        acc = acc + got[s].astype(F32)
    total[...] = acc
    rank = 64
    blocks = []
    for m in range(3):
        lo = 3 * rank + m * 16
        factor = total[m * rank : (m + 1) * rank]
        halves = []
        for parity in range(2):
            picked = total[pl.ds(lo + parity, 8, stride=2)] * weights[...]
            halves.append(_dot(picked, factor, 1, 1, precision=lax.Precision.HIGHEST))
        blocks.append(jnp.concatenate(halves, axis=1))
    sketch = (jnp.concatenate(blocks, axis=0) * scale).astype(BF)

    def body(i, carry):
        out_ref[i] = sketch
        return carry

    lax.fori_loop(0, out_ref.shape[0], body, 0, unroll=8)


def score_kernel(gathered, mine, other, scores, wide):
    groups, lines, lanes = gathered.shape
    wide[...] = gathered[...].astype(F32).reshape(groups * lines, lanes)
    acc = None
    for m in range(3):
        for h, query in enumerate((mine, other)):
            cols = [wide[pl.ds(m * 8 + h * 4 + p, groups, stride=lines)] for p in range(4)]
            block = jnp.concatenate(cols, axis=1).astype(BF)
            term = _dot(block, query[m], 1, 1)
            acc = term if acc is None else acc + term
    scores[...] = acc


def keep_kernel(chosen, valid, gathered, after, kept):
    for slot in range(kept.shape[0]):
        picked = gathered[chosen[slot]].astype(F32)
        kept[slot] = jnp.where(valid[slot] == 1, picked, 0.0).astype(BF)


def finish_kernel(parts, own, received, scores, stored):
    chips = parts.shape[0] // 2
    per_core = []
    for core in range(2):
        total = parts[core]
        for chip in range(1, chips):
            total = total + parts[2 * chip + core]
        per_core.append(total)
    for z in range(per_core[0].shape[0]):
        for core in range(2):
            scores[2 * z + core : 2 * z + core + 1] = per_core[core][z : z + 1]
    for m in range(3):
        stored[m] = (own[m].astype(F32) + received[m].astype(F32)).astype(BF)


def _vmem(n):
    return [pl.BlockSpec(memory_space=pltpu.VMEM)] * n


def local(
    layer_input,
    gate_pre,
    up_pre,
    hidden_grad,
    out_grad,
    proj_model_in,
    proj_hidden_in,
    proj_hidden_out,
    proj_model_out,
    queries,
    validity,
    owners,
):
    tokens, features = gate_pre.shape
    width = layer_input.shape[1]
    rank = proj_hidden_in.shape[1]
    seq_count, seq_len = validity.shape
    stores = lax.axis_size("store")
    groups = lax.axis_size("fsdp")
    rows = rank // stores
    capacity = 2 * seq_count
    core = lax.axis_index("store") % 2

    step = 512
    spans = len(_splits(features, step))
    lines = 3 * rank + 3 * 2 * rows
    send = pl.pallas_call(
        functools.partial(factor_kernel, stores, step),
        out_shape=jax.ShapeDtypeStruct((stores, lines, seq_len), BF),
        in_specs=[pl.BlockSpec(memory_space=pl.ANY)] * 9,
        out_specs=pl.BlockSpec(memory_space=pltpu.VMEM),
        scratch_shapes=[
            pltpu.VMEM((tokens, width), BF),
            pltpu.VMEM((features, tokens), BF),
            pltpu.VMEM((features, tokens), BF),
            pltpu.VMEM((features, tokens), BF),
            pltpu.VMEM((tokens, width), BF),
            pltpu.VMEM((width, 2 * rank), BF),
            pltpu.VMEM((rank, features), BF),
            pltpu.VMEM((features, 2 * rank), BF),
            pltpu.VMEM((rank, width), BF),
            pltpu.VMEM((features, tokens), BF),
            pltpu.VMEM((features, tokens), BF),
            pltpu.VMEM((features, tokens), BF),
            pltpu.SemaphoreType.DMA((6 + 3 * spans,)),
        ],
        compiler_params=pltpu.CompilerParams(vmem_limit_bytes=60 * 2**20),
        name="factors",
    )(
        layer_input,
        gate_pre.T,
        up_pre.T,
        hidden_grad.T,
        out_grad,
        proj_model_in,
        proj_hidden_in.T,
        proj_hidden_out,
        proj_model_out.T,
    )
    got = lax.all_to_all(send, "store", 0, 0, tiled=True)

    weights = jnp.where(core == 0, validity[0], validity[1]).astype(F32).reshape(1, seq_len)
    lines = 3 * 2 * rows * rank // 128
    spread = pl.pallas_call(
        functools.partial(sketch_kernel, float(seq_len) ** (-0.5)),
        out_shape=jax.ShapeDtypeStruct((groups, lines, 128), BF),
        in_specs=_vmem(2),
        out_specs=pl.BlockSpec(memory_space=pltpu.VMEM),
        scratch_shapes=[pltpu.VMEM(got.shape[1:], F32)],
        compiler_params=pltpu.CompilerParams(vmem_limit_bytes=8 * 2**20),
        name="sketch",
    )(got, weights)
    flip = [(s, s ^ 1) for s in range(stores)]
    query_rows = queries.transpose(1, 0, 2)
    other_rows = lax.ppermute(query_rows, "store", flip)
    gathered = lax.all_to_all(spread, "fsdp", 0, 0, tiled=True)

    own_index = lax.axis_index("fsdp")
    mine = (owners == own_index).astype(jnp.int32)
    count = owners.shape[0]
    first = lax.broadcasted_iota(jnp.int32, (count, count), 0)
    second = lax.broadcasted_iota(jnp.int32, (count, count), 1)
    slot_rank = jnp.sum(jnp.where(first < second, mine[:, None], 0), axis=0)
    slots = jnp.arange(capacity, dtype=jnp.int32)
    sequence = jnp.arange(count, dtype=jnp.int32)
    hit = (
        (slot_rank[None, :] == slots[:, None])
        & (mine[None, :] == 1)
        & (sequence[None, :] % seq_count == core)
    ).astype(jnp.int32)
    valid = jnp.sum(hit, axis=1)
    chosen = jnp.clip(jnp.sum(hit * (sequence // seq_count)[None, :], axis=1), 0, groups - 1)

    query_count = queries.shape[0]
    partial_scores = pl.pallas_call(
        score_kernel,
        out_shape=jax.ShapeDtypeStruct((groups, query_count), F32),
        in_specs=_vmem(3),
        out_specs=pl.BlockSpec(memory_space=pltpu.VMEM),
        scratch_shapes=[pltpu.VMEM((groups * lines, 128), F32)],
        compiler_params=pltpu.CompilerParams(vmem_limit_bytes=12 * 2**20),
        name="scores",
    )(gathered, query_rows, other_rows)
    kept = pl.pallas_call(
        keep_kernel,
        out_shape=jax.ShapeDtypeStruct((capacity, lines, 128), BF),
        in_specs=[pl.BlockSpec(memory_space=pltpu.SMEM)] * 2
        + _vmem(1)
        + [pl.BlockSpec(memory_space=pl.ANY)],
        out_specs=pl.BlockSpec(memory_space=pltpu.VMEM),
        cost_estimate=pl.CostEstimate(flops=0, bytes_accessed=8 * 2**20, transcendentals=0),
        compiler_params=pltpu.CompilerParams(vmem_limit_bytes=8 * 2**20),
        name="kept",
    )(chosen, valid, gathered, partial_scores)

    parts = lax.all_to_all(
        partial_scores.reshape(stores, groups // stores, query_count), "store", 0, 0, tiled=True
    )
    kept = kept.reshape(capacity, 3, 2, -1).transpose(2, 1, 0, 3)
    received = lax.ppermute(kept[1], "store", flip)
    scores, stored = pl.pallas_call(
        finish_kernel,
        out_shape=(
            jax.ShapeDtypeStruct((2 * groups // stores, query_count), F32),
            jax.ShapeDtypeStruct(kept.shape[1:], BF),
        ),
        in_specs=_vmem(3),
        out_specs=tuple(_vmem(2)),
        compiler_params=pltpu.CompilerParams(vmem_limit_bytes=8 * 2**20),
        name="finish",
    )(parts, kept[0], received)
    stored = stored.transpose(1, 0, 2)
    return (scores, stored)


def solution(mesh):
    placed = (
        P("fsdp", "store"),
        P("fsdp", "store"),
        P("fsdp", "store"),
        P("fsdp", "store"),
        P("fsdp", "store"),
        P("store", None),
        P("store", None),
        P("store", None),
        P("store", None),
        P("fsdp", None, "store"),
        P("fsdp", None),
        P(),
    )
    return jax.shard_map(
        local,
        mesh=mesh,
        in_specs=placed,
        out_specs=(P("store", "fsdp"), P("fsdp", None, "store")),
        check_vma=False,
    )
```

time: 215 us -> 65.3 us (0.30)
  waiting for transfers between devices: 151 us -> 22.6 us
  blocking collectives: 38.4 us -> 0 us
  starting transfers between devices: 0.12 us -> 33.2 us
  between operations: 13.9 us -> 0.76 us
  matrix products: 8.67 us -> 0 us
  Pallas kernels: 0 us -> 7.41 us
    reduce_scatter x2 -> x0, waiting for transfers between devices: 80 us -> none  [the longest x1 42.1 us: local(): lax.psum_scatter(partial_scores, 'store', scatter_dimension=0, tiled=True)]
    psum x1 -> x0, waiting for transfers between devices: 70.9 us -> none  [local(): in_full = lax.psum(in_part, 'store')]
    all_gather x1 -> x0, blocking collectives: 38.4 us -> none  [local(): piece = lax.all_gather(sketch_local, 'fsdp', axis=0, tiled=True)]
    all_to_all x0 -> x3, starting transfers between devices: none -> 29.1 us  [the longest x1 12 us: local(): gathered = lax.all_to_all(spread, 'fsdp', 0, 0, tiled=True)]
    all_to_all x0 -> x3, waiting for transfers between devices: none -> 21.5 us  [the longest x1 14.1 us: local(): gathered = lax.all_to_all(spread, 'fsdp', 0, 0, tiled=True)]
    dot_general x8 -> x0, matrix products: 8.67 us -> none  [the longest x1 2.23 us: local(): jnp.dot(hidden, proj_hidden_in, preferred_element_type=jnp.float32)]
    pallas_call x0 -> x5, Pallas kernels: none -> 7.41 us  [the longest x1 3.92 us: local(): pl.pallas_call(functools.partial(factor_kernel, stores, step), out_shape=...]
    ppermute x0 -> x2, starting transfers between devices: none -> 4.04 us  [the longest x1 2.02 us: local(): other_rows = lax.ppermute(query_rows, 'store', flip)]
  transfers between devices with their start and end apart: 3 -> 5, of which waited for: 3 -> 4; matrix products, arithmetic and copies ran while one was open for 2% -> 0% of each run, Pallas kernels for 0% -> 3%
where the time goes in v2:
time: 65.3 us; the launch traced here: 64.9 us
  starting transfers between devices  33.2 us (51%)
  waiting for transfers between devices  22.6 us (35%)
  Pallas kernels  7.41 us (11%)
  between operations  0.76 us (1%)
  local copies, waits for them, and re-layouts  0.72 us (1%)
    all_to_all x1, waiting for transfers between devices, local(): gathered = lax.all_to_all(spread, 'fsdp', 0, 0, tiled=True)  14.1 us
    all_to_all x1, starting transfers between devices, local(): gathered = lax.all_to_all(spread, 'fsdp', 0, 0, tiled=True)  12 us
    all_to_all x1, starting transfers between devices, local(): got = lax.all_to_all(send, 'store', 0, 0, tiled=True)  10.4 us
    all_to_all x1, starting transfers between devices, local(): lax.all_to_all(partial_scores.reshape(stores, groups // stores, query_cou...  6.76 us
    all_to_all x1, waiting for transfers between devices, local(): got = lax.all_to_all(send, 'store', 0, 0, tiled=True)  6.41 us
    pallas_call x1, Pallas kernels, local(): pl.pallas_call(functools.partial(factor_kernel, stores, step), out_shape=...  3.92 us
    ppermute x1, starting transfers between devices, local(): other_rows = lax.ppermute(query_rows, 'store', flip)  2.02 us
    ppermute x1, starting transfers between devices, local(): received = lax.ppermute(kept[1], 'store', flip)  2.02 us
  transfers between devices with their start and end apart: 5, of which 4 were waited for; matrix products, arithmetic and copies ran while one was open for 0% of the time, Pallas kernels for 3%

profile of v2, /device:TPU:1, one launch (start us, length us, event | category | flops | bytes accessed | tf_op | source)
XLA Modules:
  0.0 64.9 jit_solution(17156899277556563873)
XLA Ops:
  0.6 3.9 %factors.1 = bf16[8,240,128]{2,1,0:T(8,128)(2,1)} custom-call(bf16[256,640]{1,0:T(8,128)(2,1)} %x_hbm.1, bf16[1728,256]{1,0:T(8,128)(2,1)} %bitcast.17, bf16[1728,256]{1,0:T(8,128)(2,1)} %bitcast.18, bf16[1728,256]{1,0:T(8,128)(2,1)} %bitcast.19, bf16[256,640]{1,0:T(8,128)(2,1)} %dy_hbm.1, bf16[640,128]{1,0:T(8,128)(2,1)} %pmi_hbm.1, ...), custom_call_target="tpu_custom_call" | custom-call | tf_op jit(solution)/shard_map/factors/pallas_call | solution.py:212
  4.6 0.0 copy-start
  4.6 10.4 %all-to-all-start = ((bf16[8,240,128]{2,1,0:T(8,128)(2,1)}), bf16[8,240,128]{2,1,0:T(8,128)(2,1)S(1)}, u32[]{:S(2)}, u32[]{:S(2)}) async-start(bf16[8,240,128]{2,1,0:T(8,128)(2,1)} %factors.1), calls=%async_computation | async-start | bytes 983040 | tf_op jit(solution)/shard_map/all_to_all | solution.py:245
  15.0 0.0 copy-done
  15.0 2.0 %collective-permute-start = (bf16[3,128,512]{2,1,0:T(8,128)(2,1)S(1)}, bf16[3,128,512]{2,1,0:T(8,128)(2,1)S(1)}, u32[]{:S(2)}, u32[]{:S(2)}) collective-permute-start(bf16[3,128,512]{2,1,0:T(8,128)(2,1)S(1)} %bitcast.15), channel_id=1, source_target_pairs={{0,1},{1,0},{2,3},{3,2},{4,5},{5,4},{6,7},{7,6},{8,9},{9,8},{10,11... | collective-permute-start | bytes 1179656 | tf_op jit(solution)/shard_map/ppermute | solution.py:260
  17.0 0.0 copy-start.1
  17.0 0.7 %copy-done.1 = s32[2,128]{1,0:T(2,128)S(1)} copy-done((s32[2,128]{1,0:T(2,128)S(1)}, s32[2,128]{1,0:T(2,128)}, u32[]{:S(2)}) %copy-start.1) | copy-done | bytes 1048
  17.7 6.4 %all-to-all-done.got = bf16[8,240,128]{2,1,0:T(8,128)(2,1)S(1)} async-done(((bf16[8,240,128]{2,1,0:T(8,128)(2,1)}), bf16[8,240,128]{2,1,0:T(8,128)(2,1)S(1)}, u32[]{:S(2)}, u32[]{:S(2)}) %all-to-all-start) | async-done | bytes 491552 | tf_op jit(solution)/shard_map/all_to_all | solution.py:245
  24.1 1.3 %sketch.1 = bf16[64,24,128]{2,1,0:T(8,128)(2,1)} custom-call(bf16[8,240,128]{2,1,0:T(8,128)(2,1)S(1)} %all-to-all-done.got, f32[1,128]{1,0:T(1,128)S(1)} %fusion.2.weights), custom_call_target="tpu_custom_call" | custom-call | tf_op jit(solution)/shard_map/sketch/pallas_call | solution.py:249
  25.4 0.0 copy-start.2
  25.4 12.0 %all-to-all-start.1 = ((bf16[64,24,128]{2,1,0:T(8,128)(2,1)}), bf16[64,24,128]{2,1,0:T(8,128)(2,1)S(1)}, u32[]{:S(2)}, u32[]{:S(2)}) async-start(bf16[64,24,128]{2,1,0:T(8,128)(2,1)} %sketch.1), calls=%async_computation.1 | async-start | bytes 786432 | tf_op jit(solution)/shard_map/all_to_all | solution.py:261
  37.4 0.0 copy-done.2
  37.4 0.1 select_reduce_fusion
  37.5 0.1 convert_reduce_fusion
  37.7 0.0 collective-permute-done.other
  37.7 14.1 %all-to-all-done.1.gathered = bf16[64,24,128]{2,1,0:T(8,128)(2,1)S(1)} async-done(((bf16[64,24,128]{2,1,0:T(8,128)(2,1)}), bf16[64,24,128]{2,1,0:T(8,128)(2,1)S(1)}, u32[]{:S(2)}, u32[]{:S(2)}) %all-to-all-start.1) | async-done | bytes 393248 | tf_op jit(solution)/shard_map/all_to_all | solution.py:261
  51.8 1.0 %scores.1.after = f32[64,128]{1,0:T(8,128)} custom-call(bf16[64,24,128]{2,1,0:T(8,128)(2,1)S(1)} %all-to-all-done.1.gathered, bf16[3,128,512]{2,1,0:T(8,128)(2,1)S(1)} %bitcast.16, bf16[3,128,512]{2,1,0:T(8,128)(2,1)S(1)} %collective-permute-done.other), custom_call_target="tpu_custom_call" | custom-call | tf_op jit(solution)/shard_map/scores/pallas_call | solution.py:280
  52.8 6.8 %all-to-all-start.2 = ((f32[8,8,128]{2,1,0:T(8,128)}), f32[8,8,128]{2,1,0:T(8,128)S(1)}, u32[]{:S(2)}, u32[]{:S(2)}) async-start(f32[8,8,128]{2,1,0:T(8,128)} %bitcast.6), calls=%async_computation.2 | async-start | bytes 65536 | tf_op jit(solution)/shard_map/all_to_all | solution.py:301
  59.6 0.6 kept.1
  60.2 2.0 %collective-permute-start.1 = (bf16[3,4,512]{2,1,0:T(4,128)(2,1)S(1)}, bf16[3,4,512]{2,1,0:T(4,128)(2,1)S(1)}, u32[]{:S(2)}, u32[]{:S(2)}) collective-permute-start(bf16[3,4,512]{2,1,0:T(4,128)(2,1)S(1)} %get-tuple-element.10), channel_id=1, source_target_pairs={{0,1},{1,0},{2,3},{3,2},{4,5},{5,4},{6,7},{7,6},{8,9},{9,8},{10,11... | collective-permute-start | bytes 36872 | tf_op jit(solution)/shard_map/ppermute | solution.py:305
  62.2 1.0 %collective-permute-done.1.received = bf16[3,4,512]{2,1,0:T(4,128)(2,1)S(1)} collective-permute-done((bf16[3,4,512]{2,1,0:T(4,128)(2,1)S(1)}, bf16[3,4,512]{2,1,0:T(4,128)(2,1)S(1)}, u32[]{:S(2)}, u32[]{:S(2)}) %collective-permute-start.1) | collective-permute-done | bytes 12320 | tf_op jit(solution)/shard_map/ppermute | solution.py:305
  63.2 1.0 %all-to-all-done.2.parts = f32[8,8,128]{2,1,0:T(8,128)S(1)} async-done(((f32[8,8,128]{2,1,0:T(8,128)}), f32[8,8,128]{2,1,0:T(8,128)S(1)}, u32[]{:S(2)}, u32[]{:S(2)}) %all-to-all-start.2) | async-done | bytes 32800 | tf_op jit(solution)/shard_map/all_to_all | solution.py:301
  64.3 0.6 finish.1
  (7 shorter events, 0.1 us)
Async XLA Ops:
  4.6 10.4 %copy-start = (bf16[128,3,512]{2,0,1:T(8,128)(2,1)S(1)}, bf16[128,3,512]{2,0,1:T(8,128)(2,1)}, u32[]{:S(2)}) copy-start(bf16[128,3,512]{2,0,1:T(8,128)(2,1)} %param.21) | copy-start | bytes 1179652
  4.6 19.6 %all-to-all-start = ((bf16[8,240,128]{2,1,0:T(8,128)(2,1)}), bf16[8,240,128]{2,1,0:T(8,128)(2,1)S(1)}, u32[]{:S(2)}, u32[]{:S(2)}) async-start(bf16[8,240,128]{2,1,0:T(8,128)(2,1)} %factors.1), calls=%async_computation | async-start | bytes 983040 | tf_op jit(solution)/shard_map/all_to_all | solution.py:245
  15.0 22.7 %collective-permute-start = (bf16[3,128,512]{2,1,0:T(8,128)(2,1)S(1)}, bf16[3,128,512]{2,1,0:T(8,128)(2,1)S(1)}, u32[]{:S(2)}, u32[]{:S(2)}) collective-permute-start(bf16[3,128,512]{2,1,0:T(8,128)(2,1)S(1)} %bitcast.15), channel_id=1, source_target_pairs={{0,1},{1,0},{2,3},{3,2},{4,5},{5,4},{6,7},{7,6},{8,9},{9,8},{10,11... | collective-permute-start | bytes 1179656 | tf_op jit(solution)/shard_map/ppermute | solution.py:260
  17.0 0.7 %copy-start.1 = (s32[2,128]{1,0:T(2,128)S(1)}, s32[2,128]{1,0:T(2,128)}, u32[]{:S(2)}) copy-start(s32[2,128]{1,0:T(2,128)} %param.22) | copy-start | bytes 3076
  25.4 12.0 %copy-start.2 = (s32[128]{0:T(128)S(1)}, s32[128]{0:T(128)}, u32[]{:S(2)}) copy-start(s32[128]{0:T(128)} %param.23) | copy-start | bytes 1540
  25.4 26.3 %all-to-all-start.1 = ((bf16[64,24,128]{2,1,0:T(8,128)(2,1)}), bf16[64,24,128]{2,1,0:T(8,128)(2,1)S(1)}, u32[]{:S(2)}, u32[]{:S(2)}) async-start(bf16[64,24,128]{2,1,0:T(8,128)(2,1)} %sketch.1), calls=%async_computation.1 | async-start | bytes 786432 | tf_op jit(solution)/shard_map/all_to_all | solution.py:261
  52.8 11.5 %all-to-all-start.2 = ((f32[8,8,128]{2,1,0:T(8,128)}), f32[8,8,128]{2,1,0:T(8,128)S(1)}, u32[]{:S(2)}, u32[]{:S(2)}) async-start(f32[8,8,128]{2,1,0:T(8,128)} %bitcast.6), calls=%async_computation.2 | async-start | bytes 65536 | tf_op jit(solution)/shard_map/all_to_all | solution.py:301
  60.2 3.1 %collective-permute-start.1 = (bf16[3,4,512]{2,1,0:T(4,128)(2,1)S(1)}, bf16[3,4,512]{2,1,0:T(4,128)(2,1)S(1)}, u32[]{:S(2)}, u32[]{:S(2)}) collective-permute-start(bf16[3,4,512]{2,1,0:T(4,128)(2,1)S(1)} %get-tuple-element.10), channel_id=1, source_target_pairs={{0,1},{1,0},{2,3},{3,2},{4,5},{5,4},{6,7},{7,6},{8,9},{9,8},{10,11... | collective-permute-start | bytes 36872 | tf_op jit(solution)/shard_map/ppermute | solution.py:305

commit v3 on v2

--- a/solution.py
+++ b/solution.py
@@ -2,6 +2,7 @@
 
 import jax
 import jax.numpy as jnp
+import numpy as np
 from jax import lax
 from jax.experimental import pallas as pl
 from jax.experimental.pallas import tpu as pltpu
@@ -9,6 +10,20 @@
 
 BF = jnp.bfloat16
 F32 = jnp.float32
+GROUP_SEED = 2
+STORE_SEED = 5
+
+
+def _order(count, seed):
+    if seed is None:
+        return list(range(count))
+    return [int(i) for i in np.random.RandomState(seed).permutation(count)]
+
+
+def _exchange(x, axis, order):
+    plain = order == sorted(order)
+    groups = None if plain else [order]
+    return lax.all_to_all(x, axis, 0, 0, tiled=True, axis_index_groups=groups)
 
 
 def _dot(a, b, ca, cb, **kw):
@@ -24,6 +39,7 @@
 def factor_kernel(
     stores,
     step,
+    store_order,
     x_hbm,
     gate_hbm,
     up_hbm,
@@ -111,12 +127,13 @@
         at = slice(e * seq_len, (e + 1) * seq_len)
         factors = jnp.concatenate([from_model[:, at], in_two[:, at]], axis=0).astype(BF)
         for s in range(e, stores, 2):
-            out_ref[s, : 3 * rank] = factors
+            place = store_order.index(s)
+            out_ref[place, : 3 * rank] = factors
             for m in range(3):
                 mine = out_all[m][s * rows : (s + 1) * rows, at]
                 other = out_all[m][(s ^ 1) * rows : ((s ^ 1) + 1) * rows, at]
                 lo = 3 * rank + m * 2 * rows
-                out_ref[s, lo : lo + 2 * rows] = jnp.concatenate([mine, other], axis=0).astype(BF)
+                out_ref[place, lo : lo + 2 * rows] = jnp.concatenate([mine, other], axis=0).astype(BF)
 
 
 def sketch_kernel(scale, got, weights, out_ref, total):
@@ -144,9 +161,10 @@
     lax.fori_loop(0, out_ref.shape[0], body, 0, unroll=8)
 
 
-def score_kernel(gathered, mine, other, scores, wide):
+def score_kernel(places, gathered, mine, other, scores, wide):
     groups, lines, lanes = gathered.shape
-    wide[...] = gathered[...].astype(F32).reshape(groups * lines, lanes)
+    for i, place in enumerate(places):
+        wide[place * lines : (place + 1) * lines] = gathered[i].astype(F32)
     acc = None
     for m in range(3):
         for h, query in enumerate((mine, other)):
@@ -163,13 +181,13 @@
         kept[slot] = jnp.where(valid[slot] == 1, picked, 0.0).astype(BF)
 
 
-def finish_kernel(parts, own, received, scores, stored):
-    chips = parts.shape[0] // 2
+def finish_kernel(store_order, parts, own, received, scores, stored):
     per_core = []
     for core in range(2):
-        total = parts[core]
-        for chip in range(1, chips):
-            total = total + parts[2 * chip + core]
+        first, *others = [i for i, s in enumerate(store_order) if s % 2 == core]
+        total = parts[first]
+        for i in others:
+            total = total + parts[i]
         per_core.append(total)
     for z in range(per_core[0].shape[0]):
         for core in range(2):
@@ -205,12 +223,14 @@
     rows = rank // stores
     capacity = 2 * seq_count
     core = lax.axis_index("store") % 2
+    store_order = _order(stores, STORE_SEED)
+    group_order = _order(groups, GROUP_SEED)
 
     step = 512
     spans = len(_splits(features, step))
     lines = 3 * rank + 3 * 2 * rows
     send = pl.pallas_call(
-        functools.partial(factor_kernel, stores, step),
+        functools.partial(factor_kernel, stores, step, store_order),
         out_shape=jax.ShapeDtypeStruct((stores, lines, seq_len), BF),
         in_specs=[pl.BlockSpec(memory_space=pl.ANY)] * 9,
         out_specs=pl.BlockSpec(memory_space=pltpu.VMEM),
@@ -242,7 +262,7 @@
         proj_hidden_out,
         proj_model_out.T,
     )
-    got = lax.all_to_all(send, "store", 0, 0, tiled=True)
+    got = _exchange(send, "store", store_order)
 
     weights = jnp.where(core == 0, validity[0], validity[1]).astype(F32).reshape(1, seq_len)
     lines = 3 * 2 * rows * rank // 128
@@ -258,7 +278,7 @@
     flip = [(s, s ^ 1) for s in range(stores)]
     query_rows = queries.transpose(1, 0, 2)
     other_rows = lax.ppermute(query_rows, "store", flip)
-    gathered = lax.all_to_all(spread, "fsdp", 0, 0, tiled=True)
+    gathered = _exchange(spread, "fsdp", group_order)
 
     own_index = lax.axis_index("fsdp")
     mine = (owners == own_index).astype(jnp.int32)
@@ -267,18 +287,21 @@
     second = lax.broadcasted_iota(jnp.int32, (count, count), 1)
     slot_rank = jnp.sum(jnp.where(first < second, mine[:, None], 0), axis=0)
     slots = jnp.arange(capacity, dtype=jnp.int32)
-    sequence = jnp.arange(count, dtype=jnp.int32)
+    arrival = np.argsort(group_order).astype(np.int32)
+    sequence = np.arange(count, dtype=np.int32)
     hit = (
         (slot_rank[None, :] == slots[:, None])
         & (mine[None, :] == 1)
         & (sequence[None, :] % seq_count == core)
     ).astype(jnp.int32)
     valid = jnp.sum(hit, axis=1)
-    chosen = jnp.clip(jnp.sum(hit * (sequence // seq_count)[None, :], axis=1), 0, groups - 1)
+    chosen = jnp.clip(jnp.sum(hit * arrival[sequence // seq_count][None, :], axis=1), 0, groups - 1)
 
     query_count = queries.shape[0]
+    share = groups // stores
+    places = [store_order.index(g // share) * share + g % share for g in group_order]
     partial_scores = pl.pallas_call(
-        score_kernel,
+        functools.partial(score_kernel, places),
         out_shape=jax.ShapeDtypeStruct((groups, query_count), F32),
         in_specs=_vmem(3),
         out_specs=pl.BlockSpec(memory_space=pltpu.VMEM),
@@ -298,13 +321,13 @@
         name="kept",
     )(chosen, valid, gathered, partial_scores)
 
-    parts = lax.all_to_all(
-        partial_scores.reshape(stores, groups // stores, query_count), "store", 0, 0, tiled=True
+    parts = _exchange(
+        partial_scores.reshape(stores, share, query_count), "store", store_order
     )
     kept = kept.reshape(capacity, 3, 2, -1).transpose(2, 1, 0, 3)
     received = lax.ppermute(kept[1], "store", flip)
     scores, stored = pl.pallas_call(
-        finish_kernel,
+        functools.partial(finish_kernel, store_order),
         out_shape=(
             jax.ShapeDtypeStruct((2 * groups // stores, query_count), F32),
             jax.ShapeDtypeStruct(kept.shape[1:], BF),

time: 65.3 us -> 59.3 us (0.908)
  waiting for transfers between devices: 22.6 us -> 12.6 us
  starting transfers between devices: 33.2 us -> 35.8 us
  local copies, waits for them, and re-layouts: 0.72 us -> 2.03 us
    all_to_all x3, waiting for transfers between devices: 21.5 us -> 11.8 us  [_exchange(): return lax.all_to_all(x, axis, 0, 0, tiled=True, axis_index_groups=groups)]
    all_to_all x3, starting transfers between devices: 29.1 us -> 31.1 us  [_exchange(): return lax.all_to_all(x, axis, 0, 0, tiled=True, axis_index_groups=groups)]
    unnamed x6 -> x10, local copies, waits for them, and re-layouts: 0.68 us -> 1.99 us
  transfers between devices with their start and end apart: 5 -> 5, of which waited for: 4 -> 3; matrix products, arithmetic and copies ran while one was open for 0% -> 1% of each run, Pallas kernels for 3% -> 3%
where the time goes in v3:
time: 59.3 us; the launch traced here: 58.9 us
  starting transfers between devices  35.8 us (60%)
  waiting for transfers between devices  12.6 us (21%)
  Pallas kernels  7.38 us (12%)
  local copies, waits for them, and re-layouts  2.03 us (3%)
  between operations  0.78 us (1%)
    all_to_all x3, starting transfers between devices, _exchange(): return lax.all_to_all(x, axis, 0, 0, tiled=True, axis_index_groups=groups)  31.1 us
    all_to_all x3, waiting for transfers between devices, _exchange(): return lax.all_to_all(x, axis, 0, 0, tiled=True, axis_index_groups=groups)  11.8 us
    pallas_call x1, Pallas kernels, local(): pl.pallas_call(functools.partial(factor_kernel, stores, step, store_order...  3.91 us
    ppermute x1, starting transfers between devices, local(): received = lax.ppermute(kept[1], 'store', flip)  2.34 us
    ppermute x1, starting transfers between devices, local(): other_rows = lax.ppermute(query_rows, 'store', flip)  2.33 us
    unnamed x10, local copies, waits for them, and re-layouts  1.99 us
    pallas_call x1, Pallas kernels, local(): pl.pallas_call(functools.partial(sketch_kernel, float(seq_len) ** (-0.5))...  1.29 us
  transfers between devices with their start and end apart: 5, of which 3 were waited for; matrix products, arithmetic and copies ran while one was open for 1% of the time, Pallas kernels for 3%

profile of v3, /device:TPU:1, one launch (start us, length us, event | category | flops | bytes accessed | tf_op | source)
XLA Modules:
  0.0 58.9 jit_solution(10947024451873791393)
XLA Ops:
  0.6 3.9 %factors.1 = bf16[8,240,128]{2,1,0:T(8,128)(2,1)} custom-call(bf16[256,640]{1,0:T(8,128)(2,1)} %x_hbm.1, bf16[1728,256]{1,0:T(8,128)(2,1)} %bitcast.19, bf16[1728,256]{1,0:T(8,128)(2,1)} %bitcast.20, bf16[1728,256]{1,0:T(8,128)(2,1)} %bitcast.21, bf16[256,640]{1,0:T(8,128)(2,1)} %dy_hbm.1, bf16[640,128]{1,0:T(8,128)(2,1)} %pmi_hbm.1, ...), custom_call_target="tpu_custom_call" | custom-call | tf_op jit(solution)/shard_map/factors/pallas_call | solution.py:232
  4.6 0.0 copy-start
  4.6 10.9 %all-to-all-start = ((bf16[8,240,128]{2,1,0:T(8,128)(2,1)}), bf16[8,240,128]{2,1,0:T(8,128)(2,1)S(1)}, u32[]{:S(2)}, u32[]{:S(2)}) async-start(bf16[8,240,128]{2,1,0:T(8,128)(2,1)} %factors.1), calls=%async_computation | async-start | bytes 983040 | tf_op jit(solution)/shard_map/all_to_all | solution.py:26
  15.4 0.0 copy-done
  15.4 2.3 %collective-permute-start = (bf16[3,128,512]{2,1,0:T(8,128)(2,1)S(1)}, bf16[3,128,512]{2,1,0:T(8,128)(2,1)S(1)}, u32[]{:S(2)}, u32[]{:S(2)}) collective-permute-start(bf16[3,128,512]{2,1,0:T(8,128)(2,1)S(1)} %bitcast.17), channel_id=1, source_target_pairs={{0,1},{1,0},{2,3},{3,2},{4,5},{5,4},{6,7},{7,6},{8,9},{9,8},{10,11... | collective-permute-start | bytes 1179656 | tf_op jit(solution)/shard_map/ppermute | solution.py:280
  17.8 0.0 copy-start.1
  17.8 0.7 %copy-done.1 = s32[2,128]{1,0:T(2,128)S(1)} copy-done((s32[2,128]{1,0:T(2,128)S(1)}, s32[2,128]{1,0:T(2,128)}, u32[]{:S(2)}) %copy-start.1) | copy-done | bytes 1048
  18.5 3.8 %all-to-all-done.got = bf16[8,240,128]{2,1,0:T(8,128)(2,1)S(1)} async-done(((bf16[8,240,128]{2,1,0:T(8,128)(2,1)}), bf16[8,240,128]{2,1,0:T(8,128)(2,1)S(1)}, u32[]{:S(2)}, u32[]{:S(2)}) %all-to-all-start) | async-done | bytes 491552 | tf_op jit(solution)/shard_map/all_to_all | solution.py:26
  22.2 1.3 %sketch.1 = bf16[64,24,128]{2,1,0:T(8,128)(2,1)} custom-call(bf16[8,240,128]{2,1,0:T(8,128)(2,1)S(1)} %all-to-all-done.got, f32[1,128]{1,0:T(1,128)S(1)} %fusion.2.weights), custom_call_target="tpu_custom_call" | custom-call | tf_op jit(solution)/shard_map/sketch/pallas_call | solution.py:269
  23.5 0.0 copy-start.4
  23.5 15.3 %all-to-all-start.1 = ((bf16[64,24,128]{2,1,0:T(8,128)(2,1)}), bf16[64,24,128]{2,1,0:T(8,128)(2,1)S(1)}, u32[]{:S(2)}, u32[]{:S(2)}) async-start(bf16[64,24,128]{2,1,0:T(8,128)(2,1)} %sketch.1), calls=%async_computation.1 | async-start | bytes 786432 | tf_op jit(solution)/shard_map/all_to_all | solution.py:26
  38.8 0.0 copy-done.4
  38.8 0.0 copy-start.2
  38.8 0.6 %copy-done.2 = s32[128]{0:T(128)S(1)} copy-done((s32[128]{0:T(128)S(1)}, s32[128]{0:T(128)}, u32[]{:S(2)}) %copy-start.2) | copy-done | bytes 536
  39.5 0.1 select_reduce_fusion
  39.6 0.0 copy-start.3
  39.6 0.7 %copy-done.3 = s32[128]{0:T(128)S(1)} copy-done((s32[128]{0:T(128)S(1)}, s32[128]{0:T(128)}, u32[]{:S(2)}) %copy-start.3) | copy-done | bytes 536
  40.3 0.1 convert_reduce_fusion
  40.4 0.0 collective-permute-done.other
  40.4 8.1 %all-to-all-done.1.gathered = bf16[64,24,128]{2,1,0:T(8,128)(2,1)S(1)} async-done(((bf16[64,24,128]{2,1,0:T(8,128)(2,1)}), bf16[64,24,128]{2,1,0:T(8,128)(2,1)S(1)}, u32[]{:S(2)}, u32[]{:S(2)}) %all-to-all-start.1) | async-done | bytes 393248 | tf_op jit(solution)/shard_map/all_to_all | solution.py:26
  48.5 1.0 %scores.1.after = f32[64,128]{1,0:T(8,128)} custom-call(bf16[64,24,128]{2,1,0:T(8,128)(2,1)S(1)} %all-to-all-done.1.gathered, bf16[3,128,512]{2,1,0:T(8,128)(2,1)S(1)} %bitcast.18, bf16[3,128,512]{2,1,0:T(8,128)(2,1)S(1)} %collective-permute-done.other), custom_call_target="tpu_custom_call" | custom-call | tf_op jit(solution)/shard_map/scores/pallas_call | solution.py:303
  49.5 5.0 %all-to-all-start.2 = ((f32[8,8,128]{2,1,0:T(8,128)}), f32[8,8,128]{2,1,0:T(8,128)S(1)}, u32[]{:S(2)}, u32[]{:S(2)}) async-start(f32[8,8,128]{2,1,0:T(8,128)} %bitcast.6), calls=%async_computation.2 | async-start | bytes 65536 | tf_op jit(solution)/shard_map/all_to_all | solution.py:26
  54.5 0.6 kept.1
  55.1 2.3 %collective-permute-start.1 = (bf16[3,4,512]{2,1,0:T(4,128)(2,1)S(1)}, bf16[3,4,512]{2,1,0:T(4,128)(2,1)S(1)}, u32[]{:S(2)}, u32[]{:S(2)}) collective-permute-start(bf16[3,4,512]{2,1,0:T(4,128)(2,1)S(1)} %get-tuple-element.10), channel_id=1, source_target_pairs={{0,1},{1,0},{2,3},{3,2},{4,5},{5,4},{6,7},{7,6},{8,9},{9,8},{10,11... | collective-permute-start | bytes 36872 | tf_op jit(solution)/shard_map/ppermute | solution.py:328
  57.5 0.8 %collective-permute-done.1.received = bf16[3,4,512]{2,1,0:T(4,128)(2,1)S(1)} collective-permute-done((bf16[3,4,512]{2,1,0:T(4,128)(2,1)S(1)}, bf16[3,4,512]{2,1,0:T(4,128)(2,1)S(1)}, u32[]{:S(2)}, u32[]{:S(2)}) %collective-permute-start.1) | collective-permute-done | bytes 12320 | tf_op jit(solution)/shard_map/ppermute | solution.py:328
  58.3 0.0 all-to-all-done.2.parts
  58.3 0.6 %finish.1 = (f32[16,128]{1,0:T(8,128)}, bf16[3,4,512]{2,1,0:T(4,128)(2,1)}) custom-call(f32[8,8,128]{2,1,0:T(8,128)S(1)} %all-to-all-done.2.parts, bf16[3,4,512]{2,1,0:T(4,128)(2,1)S(1)} %get-tuple-element.11.own, bf16[3,4,512]{2,1,0:T(4,128)(2,1)S(1)} %collective-permute-done.1.received), custom_call_target="tpu_custom_call" | custom-call | tf_op jit(solution)/shard_map/finish/pallas_call | solution.py:329
  (7 shorter events, 0.1 us)
Async XLA Ops:
  4.6 10.9 %copy-start = (bf16[128,3,512]{2,0,1:T(8,128)(2,1)S(1)}, bf16[128,3,512]{2,0,1:T(8,128)(2,1)}, u32[]{:S(2)}) copy-start(bf16[128,3,512]{2,0,1:T(8,128)(2,1)} %param.23) | copy-start | bytes 1179652
  4.6 17.7 %all-to-all-start = ((bf16[8,240,128]{2,1,0:T(8,128)(2,1)}), bf16[8,240,128]{2,1,0:T(8,128)(2,1)S(1)}, u32[]{:S(2)}, u32[]{:S(2)}) async-start(bf16[8,240,128]{2,1,0:T(8,128)(2,1)} %factors.1), calls=%async_computation | async-start | bytes 983040 | tf_op jit(solution)/shard_map/all_to_all | solution.py:26
  15.4 25.0 %collective-permute-start = (bf16[3,128,512]{2,1,0:T(8,128)(2,1)S(1)}, bf16[3,128,512]{2,1,0:T(8,128)(2,1)S(1)}, u32[]{:S(2)}, u32[]{:S(2)}) collective-permute-start(bf16[3,128,512]{2,1,0:T(8,128)(2,1)S(1)} %bitcast.17), channel_id=1, source_target_pairs={{0,1},{1,0},{2,3},{3,2},{4,5},{5,4},{6,7},{7,6},{8,9},{9,8},{10,11... | collective-permute-start | bytes 1179656 | tf_op jit(solution)/shard_map/ppermute | solution.py:280
  17.8 0.7 %copy-start.1 = (s32[2,128]{1,0:T(2,128)S(1)}, s32[2,128]{1,0:T(2,128)}, u32[]{:S(2)}) copy-start(s32[2,128]{1,0:T(2,128)} %param.24) | copy-start | bytes 3076
  23.5 15.3 %copy-start.4 = (s32[1,128]{1,0:T(1,128)S(1)}, s32[1,128]{1,0:T(1,128)}, u32[]{:S(2)}) copy-start(s32[1,128]{1,0:T(1,128)} %constant.31.clone) | copy-start | bytes 1540
  23.5 25.0 %all-to-all-start.1 = ((bf16[64,24,128]{2,1,0:T(8,128)(2,1)}), bf16[64,24,128]{2,1,0:T(8,128)(2,1)S(1)}, u32[]{:S(2)}, u32[]{:S(2)}) async-start(bf16[64,24,128]{2,1,0:T(8,128)(2,1)} %sketch.1), calls=%async_computation.1 | async-start | bytes 786432 | tf_op jit(solution)/shard_map/all_to_all | solution.py:26
  38.8 0.7 %copy-start.2 = (s32[128]{0:T(128)S(1)}, s32[128]{0:T(128)}, u32[]{:S(2)}) copy-start(s32[128]{0:T(128)} %param.25) | copy-start | bytes 1540
  39.6 0.7 %copy-start.3 = (s32[128]{0:T(128)S(1)}, s32[128]{0:T(128)}, u32[]{:S(2)}) copy-start(s32[128]{0:T(128)} %constant.34) | copy-start | bytes 1540
  49.5 8.8 %all-to-all-start.2 = ((f32[8,8,128]{2,1,0:T(8,128)}), f32[8,8,128]{2,1,0:T(8,128)S(1)}, u32[]{:S(2)}, u32[]{:S(2)}) async-start(f32[8,8,128]{2,1,0:T(8,128)} %bitcast.6), calls=%async_computation.2 | async-start | bytes 65536 | tf_op jit(solution)/shard_map/all_to_all | solution.py:26
  55.1 3.2 %collective-permute-start.1 = (bf16[3,4,512]{2,1,0:T(4,128)(2,1)S(1)}, bf16[3,4,512]{2,1,0:T(4,128)(2,1)S(1)}, u32[]{:S(2)}, u32[]{:S(2)}) collective-permute-start(bf16[3,4,512]{2,1,0:T(4,128)(2,1)S(1)} %get-tuple-element.10), channel_id=1, source_target_pairs={{0,1},{1,0},{2,3},{3,2},{4,5},{5,4},{6,7},{7,6},{8,9},{9,8},{10,11... | collective-permute-start | bytes 36872 | tf_op jit(solution)/shard_map/ppermute | solution.py:328

commit v4 on v3

--- a/solution.py
+++ b/solution.py
@@ -11,7 +11,7 @@
 BF = jnp.bfloat16
 F32 = jnp.float32
 GROUP_SEED = 2
-STORE_SEED = 5
+STORE_SEED = 8
 
 
 def _order(count, seed):
@@ -136,7 +136,7 @@
                 out_ref[place, lo : lo + 2 * rows] = jnp.concatenate([mine, other], axis=0).astype(BF)
 
 
-def sketch_kernel(scale, got, weights, out_ref, total):
+def sketch_kernel(scale, got, weights, chooser, out_ref, total):
     stores = got.shape[0]
     acc = got[0].astype(F32)
     for s in range(1, stores):
@@ -147,11 +147,10 @@
     for m in range(3):
         lo = 3 * rank + m * 16
         factor = total[m * rank : (m + 1) * rank]
-        halves = []
-        for parity in range(2):
-            picked = total[pl.ds(lo + parity, 8, stride=2)] * weights[...]
-            halves.append(_dot(picked, factor, 1, 1, precision=lax.Precision.HIGHEST))
-        blocks.append(jnp.concatenate(halves, axis=1))
+        picked = [total[pl.ds(lo + parity, 8, stride=2)] for parity in range(2)]
+        picked = jnp.concatenate(picked, axis=0) * weights[...]
+        both = _dot(picked, factor, 1, 1, precision=lax.Precision.HIGHEST)
+        blocks.append(jnp.concatenate([both[:8], both[8:]], axis=1))
     sketch = (jnp.concatenate(blocks, axis=0) * scale).astype(BF)
 
     def body(i, carry):
@@ -161,24 +160,20 @@
     lax.fori_loop(0, out_ref.shape[0], body, 0, unroll=8)
 
 
-def score_kernel(places, gathered, mine, other, scores, wide):
+def score_kernel(places, gathered, mine, other, chooser, scores, kept, passed, wide):
     groups, lines, lanes = gathered.shape
+    capacity = kept.shape[1]
     for i, place in enumerate(places):
         wide[place * lines : (place + 1) * lines] = gathered[i].astype(F32)
     acc = None
     for m in range(3):
-        for h, query in enumerate((mine, other)):
+        for h, (query, held) in enumerate(((mine, kept), (other, passed))):
             cols = [wide[pl.ds(m * 8 + h * 4 + p, groups, stride=lines)] for p in range(4)]
             block = jnp.concatenate(cols, axis=1).astype(BF)
             term = _dot(block, query[m], 1, 1)
             acc = term if acc is None else acc + term
+            held[m] = _dot(chooser[...], block, 1, 0)[:capacity].astype(BF)
     scores[...] = acc
-
-
-def keep_kernel(chosen, valid, gathered, after, kept):
-    for slot in range(kept.shape[0]):
-        picked = gathered[chosen[slot]].astype(F32)
-        kept[slot] = jnp.where(valid[slot] == 1, picked, 0.0).astype(BF)
 
 
 def finish_kernel(store_order, parts, own, received, scores, stored):
@@ -264,79 +259,67 @@
     )
     got = _exchange(send, "store", store_order)
 
-    weights = jnp.where(core == 0, validity[0], validity[1]).astype(F32).reshape(1, seq_len)
-    lines = 3 * 2 * rows * rank // 128
-    spread = pl.pallas_call(
-        functools.partial(sketch_kernel, float(seq_len) ** (-0.5)),
-        out_shape=jax.ShapeDtypeStruct((groups, lines, 128), BF),
-        in_specs=_vmem(2),
-        out_specs=pl.BlockSpec(memory_space=pltpu.VMEM),
-        scratch_shapes=[pltpu.VMEM(got.shape[1:], F32)],
-        compiler_params=pltpu.CompilerParams(vmem_limit_bytes=8 * 2**20),
-        name="sketch",
-    )(got, weights)
-    flip = [(s, s ^ 1) for s in range(stores)]
-    query_rows = queries.transpose(1, 0, 2)
-    other_rows = lax.ppermute(query_rows, "store", flip)
-    gathered = _exchange(spread, "fsdp", group_order)
-
+    share = groups // stores
+    places = [store_order.index(g // share) * share + g % share for g in group_order]
+    at_place = np.argsort([store_order.index(g // share) * share + g % share for g in range(groups)])
     own_index = lax.axis_index("fsdp")
     mine = (owners == own_index).astype(jnp.int32)
     count = owners.shape[0]
     first = lax.broadcasted_iota(jnp.int32, (count, count), 0)
     second = lax.broadcasted_iota(jnp.int32, (count, count), 1)
     slot_rank = jnp.sum(jnp.where(first < second, mine[:, None], 0), axis=0)
-    slots = jnp.arange(capacity, dtype=jnp.int32)
-    arrival = np.argsort(group_order).astype(np.int32)
-    sequence = np.arange(count, dtype=np.int32)
-    hit = (
-        (slot_rank[None, :] == slots[:, None])
-        & (mine[None, :] == 1)
-        & (sequence[None, :] % seq_count == core)
-    ).astype(jnp.int32)
-    valid = jnp.sum(hit, axis=1)
-    chosen = jnp.clip(jnp.sum(hit * arrival[sequence // seq_count][None, :], axis=1), 0, groups - 1)
+    slots = jnp.arange(8, dtype=jnp.int32)
+    hit = ((slot_rank[None, :] == slots[:, None]) & (mine[None, :] == 1)).astype(BF)
+    wanted = jnp.asarray(seq_count * at_place.astype(np.int32)) + core
+    chooser = jnp.dot(
+        hit,
+        (jnp.arange(count, dtype=jnp.int32)[:, None] == wanted[None, :]).astype(BF),
+        preferred_element_type=F32,
+    ).astype(BF)
+
+    weights = jnp.where(core == 0, validity[0], validity[1]).astype(F32).reshape(1, seq_len)
+    lines = 3 * 2 * rows * rank // 128
+    spread = pl.pallas_call(
+        functools.partial(sketch_kernel, float(seq_len) ** (-0.5)),
+        out_shape=jax.ShapeDtypeStruct((groups, lines, 128), BF),
+        in_specs=_vmem(2) + [pl.BlockSpec(memory_space=pl.ANY)],
+        out_specs=pl.BlockSpec(memory_space=pltpu.VMEM),
+        scratch_shapes=[pltpu.VMEM(got.shape[1:], F32)],
+        compiler_params=pltpu.CompilerParams(vmem_limit_bytes=8 * 2**20),
+        name="sketch",
+    )(got, weights, chooser)
+    flip = [(s, s ^ 1) for s in range(stores)]
+    query_rows = queries.transpose(1, 0, 2)
+    other_rows = lax.ppermute(query_rows, "store", flip)
+    gathered = _exchange(spread, "fsdp", group_order)
 
     query_count = queries.shape[0]
-    share = groups // stores
-    places = [store_order.index(g // share) * share + g % share for g in group_order]
-    partial_scores = pl.pallas_call(
+    held = jax.ShapeDtypeStruct((3, capacity, rows * rank), BF)
+    partial_scores, kept, passed = pl.pallas_call(
         functools.partial(score_kernel, places),
-        out_shape=jax.ShapeDtypeStruct((groups, query_count), F32),
-        in_specs=_vmem(3),
-        out_specs=pl.BlockSpec(memory_space=pltpu.VMEM),
+        out_shape=(jax.ShapeDtypeStruct((groups, query_count), F32), held, held),
+        in_specs=_vmem(4),
+        out_specs=tuple(_vmem(3)),
         scratch_shapes=[pltpu.VMEM((groups * lines, 128), F32)],
         compiler_params=pltpu.CompilerParams(vmem_limit_bytes=12 * 2**20),
         name="scores",
-    )(gathered, query_rows, other_rows)
-    kept = pl.pallas_call(
-        keep_kernel,
-        out_shape=jax.ShapeDtypeStruct((capacity, lines, 128), BF),
-        in_specs=[pl.BlockSpec(memory_space=pltpu.SMEM)] * 2
-        + _vmem(1)
-        + [pl.BlockSpec(memory_space=pl.ANY)],
-        out_specs=pl.BlockSpec(memory_space=pltpu.VMEM),
-        cost_estimate=pl.CostEstimate(flops=0, bytes_accessed=8 * 2**20, transcendentals=0),
-        compiler_params=pltpu.CompilerParams(vmem_limit_bytes=8 * 2**20),
-        name="kept",
-    )(chosen, valid, gathered, partial_scores)
+    )(gathered, query_rows, other_rows, chooser)
 
     parts = _exchange(
         partial_scores.reshape(stores, share, query_count), "store", store_order
     )
-    kept = kept.reshape(capacity, 3, 2, -1).transpose(2, 1, 0, 3)
-    received = lax.ppermute(kept[1], "store", flip)
+    received = lax.ppermute(passed, "store", flip)
     scores, stored = pl.pallas_call(
         functools.partial(finish_kernel, store_order),
         out_shape=(
             jax.ShapeDtypeStruct((2 * groups // stores, query_count), F32),
-            jax.ShapeDtypeStruct(kept.shape[1:], BF),
+            held,
         ),
         in_specs=_vmem(3),
         out_specs=tuple(_vmem(2)),
         compiler_params=pltpu.CompilerParams(vmem_limit_bytes=8 * 2**20),
         name="finish",
-    )(parts, kept[0], received)
+    )(parts, kept, received)
     stored = stored.transpose(1, 0, 2)
     return (scores, stored)
 

time: 59.3 us -> 58.2 us (0.981)
  Pallas kernels: 7.38 us -> 6.77 us
    all_to_all x3, waiting for transfers between devices: 11.8 us -> 10.2 us  [_exchange(): return lax.all_to_all(x, axis, 0, 0, tiled=True, axis_index_groups=groups)]
    ppermute x1, waiting for transfers between devices: 0.01 us -> 1.33 us  [local(): other_rows = lax.ppermute(query_rows, 'store', flip)]
    pallas_call x2 -> x1, Pallas kernels: 1.56 us -> 1.09 us  [local(): pl.pallas_call(functools.partial(score_kernel, places), out_shape=(jax.Sh...]
    unnamed x10 -> x8, local copies, waits for them, and re-layouts: 1.99 us -> 1.89 us
  transfers between devices with their start and end apart: 5 -> 5, of which waited for: 3 -> 5; matrix products, arithmetic and copies ran while one was open for 1% -> 0% of each run, Pallas kernels for 3% -> 0%
where the time goes in v4:
time: 58.2 us; the launch traced here: 57.8 us
  starting transfers between devices  35.8 us (62%)
  waiting for transfers between devices  12.4 us (21%)
  Pallas kernels  6.77 us (12%)
  local copies, waits for them, and re-layouts  1.89 us (3%)
  between operations  0.68 us (1%)
    all_to_all x3, starting transfers between devices, _exchange(): return lax.all_to_all(x, axis, 0, 0, tiled=True, axis_index_groups=groups)  31 us
    all_to_all x3, waiting for transfers between devices, _exchange(): return lax.all_to_all(x, axis, 0, 0, tiled=True, axis_index_groups=groups)  10.2 us
    pallas_call x1, Pallas kernels, local(): pl.pallas_call(functools.partial(factor_kernel, stores, step, store_order...  3.93 us
    ppermute x1, starting transfers between devices, local(): other_rows = lax.ppermute(query_rows, 'store', flip)  2.5 us
    ppermute x1, starting transfers between devices, local(): received = lax.ppermute(passed, 'store', flip)  2.25 us
    unnamed x8, local copies, waits for them, and re-layouts  1.89 us
    ppermute x1, waiting for transfers between devices, local(): other_rows = lax.ppermute(query_rows, 'store', flip)  1.33 us
  transfers between devices with their start and end apart: 5, of which 5 were waited for; matrix products, arithmetic and copies ran while one was open for 0% of the time, Pallas kernels for 0%

profile of v4, /device:TPU:1, one launch (start us, length us, event | category | flops | bytes accessed | tf_op | source)
XLA Modules:
  0.0 57.8 jit_solution(12489895257087989839)
XLA Ops:
  0.6 3.9 %factors.1 = bf16[8,240,128]{2,1,0:T(8,128)(2,1)} custom-call(bf16[256,640]{1,0:T(8,128)(2,1)} %x_hbm.1, bf16[1728,256]{1,0:T(8,128)(2,1)} %bitcast.10, bf16[1728,256]{1,0:T(8,128)(2,1)} %bitcast.11, bf16[1728,256]{1,0:T(8,128)(2,1)} %bitcast.12, bf16[256,640]{1,0:T(8,128)(2,1)} %dy_hbm.1, bf16[640,128]{1,0:T(8,128)(2,1)} %pmi_hbm.1, ...), custom_call_target="tpu_custom_call" | custom-call | tf_op jit(solution)/shard_map/factors/pallas_call | solution.py:227
  4.6 10.8 %all-to-all-start = ((bf16[8,240,128]{2,1,0:T(8,128)(2,1)}), bf16[8,240,128]{2,1,0:T(8,128)(2,1)S(1)}, u32[]{:S(2)}, u32[]{:S(2)}) async-start(bf16[8,240,128]{2,1,0:T(8,128)(2,1)} %factors.1), calls=%async_computation | async-start | bytes 983040 | tf_op jit(solution)/shard_map/all_to_all | solution.py:26
  15.3 0.0 copy-start.2
  15.3 0.7 %copy-done.2 = s32[128]{0:T(128)S(1)} copy-done((s32[128]{0:T(128)S(1)}, s32[128]{0:T(128)}, u32[]{:S(2)}) %copy-start.2) | copy-done | bytes 536
  16.0 0.0 copy-start.1
  16.0 0.1 select_reduce_fusion
  16.1 0.6 %copy-done.1 = s32[2,128]{1,0:T(2,128)S(1)} copy-done((s32[2,128]{1,0:T(2,128)S(1)}, s32[2,128]{1,0:T(2,128)}, u32[]{:S(2)}) %copy-start.1) | copy-done | bytes 1048
  16.7 0.0 copy-start.3
  16.7 0.6 %copy-done.3 = s32[64]{0:T(128)S(1)} copy-done((s32[64]{0:T(128)S(1)}, s32[64]{0:T(128)}, u32[]{:S(2)}) %copy-start.3) | copy-done | bytes 280
  17.3 0.1 convolution_convert_fusion.chooser
  17.5 4.3 %all-to-all-done.got = bf16[8,240,128]{2,1,0:T(8,128)(2,1)S(1)} async-done(((bf16[8,240,128]{2,1,0:T(8,128)(2,1)}), bf16[8,240,128]{2,1,0:T(8,128)(2,1)S(1)}, u32[]{:S(2)}, u32[]{:S(2)}) %all-to-all-start) | async-done | bytes 491552 | tf_op jit(solution)/shard_map/all_to_all | solution.py:26
  21.7 1.1 %sketch.1 = bf16[64,24,128]{2,1,0:T(8,128)(2,1)} custom-call(bf16[8,240,128]{2,1,0:T(8,128)(2,1)S(1)} %all-to-all-done.got, f32[1,128]{1,0:T(1,128)S(1)} %fusion.5.weights, bf16[8,64]{1,0:T(8,128)(2,1)S(1)} %convolution_convert_fusion.chooser), custom_call_target="tpu_custom_call" | custom-call | tf_op jit(solution)/shard_map/sketch/pallas_call | solution.py:282
  22.9 0.0 copy-start
  22.9 15.4 %all-to-all-start.1 = ((bf16[64,24,128]{2,1,0:T(8,128)(2,1)}), bf16[64,24,128]{2,1,0:T(8,128)(2,1)S(1)}, u32[]{:S(2)}, u32[]{:S(2)}) async-start(bf16[64,24,128]{2,1,0:T(8,128)(2,1)} %sketch.1), calls=%async_computation.1 | async-start | bytes 786432 | tf_op jit(solution)/shard_map/all_to_all | solution.py:26
  38.2 0.0 copy-done
  38.2 2.5 %collective-permute-start = (bf16[3,128,512]{2,1,0:T(8,128)(2,1)S(1)}, bf16[3,128,512]{2,1,0:T(8,128)(2,1)S(1)}, u32[]{:S(2)}, u32[]{:S(2)}) collective-permute-start(bf16[3,128,512]{2,1,0:T(8,128)(2,1)S(1)} %bitcast.8), channel_id=1, source_target_pairs={{0,1},{1,0},{2,3},{3,2},{4,5},{5,4},{6,7},{7,6},{8,9},{9,8},{10,11... | collective-permute-start | bytes 1179656 | tf_op jit(solution)/shard_map/ppermute | solution.py:293
  40.8 1.3 %collective-permute-done.other = bf16[3,128,512]{2,1,0:T(8,128)(2,1)S(1)} collective-permute-done((bf16[3,128,512]{2,1,0:T(8,128)(2,1)S(1)}, bf16[3,128,512]{2,1,0:T(8,128)(2,1)S(1)}, u32[]{:S(2)}, u32[]{:S(2)}) %collective-permute-start) | collective-permute-done | bytes 393248 | tf_op jit(solution)/shard_map/ppermute | solution.py:293
  42.1 5.8 %all-to-all-done.1.gathered = bf16[64,24,128]{2,1,0:T(8,128)(2,1)S(1)} async-done(((bf16[64,24,128]{2,1,0:T(8,128)(2,1)}), bf16[64,24,128]{2,1,0:T(8,128)(2,1)S(1)}, u32[]{:S(2)}, u32[]{:S(2)}) %all-to-all-start.1) | async-done | bytes 393248 | tf_op jit(solution)/shard_map/all_to_all | solution.py:26
  47.9 1.1 %scores.1 = (f32[64,128]{1,0:T(8,128)}, bf16[3,4,512]{2,1,0:T(4,128)(2,1)S(1)}, bf16[3,4,512]{2,1,0:T(4,128)(2,1)S(1)}) custom-call(bf16[64,24,128]{2,1,0:T(8,128)(2,1)S(1)} %all-to-all-done.1.gathered, bf16[3,128,512]{2,1,0:T(8,128)(2,1)S(1)} %bitcast.9, bf16[3,128,512]{2,1,0:T(8,128)(2,1)S(1)} %collective-permute-done.other, ...), custom_call_target="tpu_custom_call" | custom-call | tf_op jit(solution)/shard_map/scores/pallas_call | solution.py:298
  49.0 4.9 %all-to-all-start.2 = ((f32[8,8,128]{2,1,0:T(8,128)}), f32[8,8,128]{2,1,0:T(8,128)S(1)}, u32[]{:S(2)}, u32[]{:S(2)}) async-start(f32[8,8,128]{2,1,0:T(8,128)} %bitcast.6), calls=%async_computation.2 | async-start | bytes 65536 | tf_op jit(solution)/shard_map/all_to_all | solution.py:26
  53.9 2.2 %collective-permute-start.1 = (bf16[3,4,512]{2,1,0:T(4,128)(2,1)S(1)}, bf16[3,4,512]{2,1,0:T(4,128)(2,1)S(1)}, u32[]{:S(2)}, u32[]{:S(2)}) collective-permute-start(bf16[3,4,512]{2,1,0:T(4,128)(2,1)S(1)} %get-tuple-element.9), channel_id=1, source_target_pairs={{0,1},{1,0},{2,3},{3,2},{4,5},{5,4},{6,7},{7,6},{8,9},{9,8},{10,11... | collective-permute-start | bytes 36872 | tf_op jit(solution)/shard_map/ppermute | solution.py:311
  56.2 0.8 %collective-permute-done.1.received = bf16[3,4,512]{2,1,0:T(4,128)(2,1)S(1)} collective-permute-done((bf16[3,4,512]{2,1,0:T(4,128)(2,1)S(1)}, bf16[3,4,512]{2,1,0:T(4,128)(2,1)S(1)}, u32[]{:S(2)}, u32[]{:S(2)}) %collective-permute-start.1) | collective-permute-done | bytes 12320 | tf_op jit(solution)/shard_map/ppermute | solution.py:311
  57.0 0.1 all-to-all-done.2.parts
  57.1 0.6 %finish.1 = (f32[16,128]{1,0:T(8,128)}, bf16[3,4,512]{2,1,0:T(4,128)(2,1)}) custom-call(f32[8,8,128]{2,1,0:T(8,128)S(1)} %all-to-all-done.2.parts, bf16[3,4,512]{2,1,0:T(4,128)(2,1)S(1)} %get-tuple-element.8.own, bf16[3,4,512]{2,1,0:T(4,128)(2,1)S(1)} %collective-permute-done.1.received), custom_call_target="tpu_custom_call" | custom-call | tf_op jit(solution)/shard_map/finish/pallas_call | solution.py:312
  (3 shorter events, 0.0 us)
Async XLA Ops:
  4.6 17.2 %all-to-all-start = ((bf16[8,240,128]{2,1,0:T(8,128)(2,1)}), bf16[8,240,128]{2,1,0:T(8,128)(2,1)S(1)}, u32[]{:S(2)}, u32[]{:S(2)}) async-start(bf16[8,240,128]{2,1,0:T(8,128)(2,1)} %factors.1), calls=%async_computation | async-start | bytes 983040 | tf_op jit(solution)/shard_map/all_to_all | solution.py:26
  15.3 0.7 %copy-start.2 = (s32[128]{0:T(128)S(1)}, s32[128]{0:T(128)}, u32[]{:S(2)}) copy-start(s32[128]{0:T(128)} %param.24) | copy-start | bytes 1540
  16.0 0.7 %copy-start.1 = (s32[2,128]{1,0:T(2,128)S(1)}, s32[2,128]{1,0:T(2,128)}, u32[]{:S(2)}) copy-start(s32[2,128]{1,0:T(2,128)} %param.23) | copy-start | bytes 3076
  16.7 0.7 %copy-start.3 = (s32[64]{0:T(128)S(1)}, s32[64]{0:T(128)}, u32[]{:S(2)}) copy-start(s32[64]{0:T(128)} %constant.26.clone) | copy-start | bytes 772
  22.9 15.4 %copy-start = (bf16[128,3,512]{2,0,1:T(8,128)(2,1)S(1)}, bf16[128,3,512]{2,0,1:T(8,128)(2,1)}, u32[]{:S(2)}) copy-start(bf16[128,3,512]{2,0,1:T(8,128)(2,1)} %param.22) | copy-start | bytes 1179652
  22.9 25.1 %all-to-all-start.1 = ((bf16[64,24,128]{2,1,0:T(8,128)(2,1)}), bf16[64,24,128]{2,1,0:T(8,128)(2,1)S(1)}, u32[]{:S(2)}, u32[]{:S(2)}) async-start(bf16[64,24,128]{2,1,0:T(8,128)(2,1)} %sketch.1), calls=%async_computation.1 | async-start | bytes 786432 | tf_op jit(solution)/shard_map/all_to_all | solution.py:26
  38.2 3.8 %collective-permute-start = (bf16[3,128,512]{2,1,0:T(8,128)(2,1)S(1)}, bf16[3,128,512]{2,1,0:T(8,128)(2,1)S(1)}, u32[]{:S(2)}, u32[]{:S(2)}) collective-permute-start(bf16[3,128,512]{2,1,0:T(8,128)(2,1)S(1)} %bitcast.8), channel_id=1, source_target_pairs={{0,1},{1,0},{2,3},{3,2},{4,5},{5,4},{6,7},{7,6},{8,9},{9,8},{10,11... | collective-permute-start | bytes 1179656 | tf_op jit(solution)/shard_map/ppermute | solution.py:293
  49.0 8.1 %all-to-all-start.2 = ((f32[8,8,128]{2,1,0:T(8,128)}), f32[8,8,128]{2,1,0:T(8,128)S(1)}, u32[]{:S(2)}, u32[]{:S(2)}) async-start(f32[8,8,128]{2,1,0:T(8,128)} %bitcast.6), calls=%async_computation.2 | async-start | bytes 65536 | tf_op jit(solution)/shard_map/all_to_all | solution.py:26
  53.9 3.1 %collective-permute-start.1 = (bf16[3,4,512]{2,1,0:T(4,128)(2,1)S(1)}, bf16[3,4,512]{2,1,0:T(4,128)(2,1)S(1)}, u32[]{:S(2)}, u32[]{:S(2)}) collective-permute-start(bf16[3,4,512]{2,1,0:T(4,128)(2,1)S(1)} %get-tuple-element.9), channel_id=1, source_target_pairs={{0,1},{1,0},{2,3},{3,2},{4,5},{5,4},{6,7},{7,6},{8,9},{9,8},{10,11... | collective-permute-start | bytes 36872 | tf_op jit(solution)/shard_map/ppermute | solution.py:311

commit v5 on v4

--- a/solution.py
+++ b/solution.py
@@ -136,7 +136,7 @@
                 out_ref[place, lo : lo + 2 * rows] = jnp.concatenate([mine, other], axis=0).astype(BF)
 
 
-def sketch_kernel(scale, got, weights, chooser, out_ref, total):
+def sketch_kernel(scale, got, weights, chooser, other, out_ref, total):
     stores = got.shape[0]
     acc = got[0].astype(F32)
     for s in range(1, stores):
@@ -277,20 +277,20 @@
         preferred_element_type=F32,
     ).astype(BF)
 
+    flip = [(s, s ^ 1) for s in range(stores)]
+    query_rows = queries.transpose(1, 0, 2)
+    other_rows = lax.ppermute(query_rows, "store", flip)
     weights = jnp.where(core == 0, validity[0], validity[1]).astype(F32).reshape(1, seq_len)
     lines = 3 * 2 * rows * rank // 128
     spread = pl.pallas_call(
         functools.partial(sketch_kernel, float(seq_len) ** (-0.5)),
         out_shape=jax.ShapeDtypeStruct((groups, lines, 128), BF),
-        in_specs=_vmem(2) + [pl.BlockSpec(memory_space=pl.ANY)],
+        in_specs=_vmem(2) + [pl.BlockSpec(memory_space=pl.ANY)] * 2,
         out_specs=pl.BlockSpec(memory_space=pltpu.VMEM),
         scratch_shapes=[pltpu.VMEM(got.shape[1:], F32)],
         compiler_params=pltpu.CompilerParams(vmem_limit_bytes=8 * 2**20),
         name="sketch",
-    )(got, weights, chooser)
-    flip = [(s, s ^ 1) for s in range(stores)]
-    query_rows = queries.transpose(1, 0, 2)
-    other_rows = lax.ppermute(query_rows, "store", flip)
+    )(got, weights, chooser, other_rows)
     gathered = _exchange(spread, "fsdp", group_order)
 
     query_count = queries.shape[0]

time: 58.2 us -> 57.2 us (0.983)
  blocking collectives: 0 us -> 24.7 us
  starting transfers between devices: 35.8 us -> 20.4 us
  waiting for transfers between devices: 12.4 us -> 2.72 us
  Pallas kernels: 6.77 us -> 6.02 us
    all_to_all x0 -> x1, blocking collectives: none -> 24.7 us  [_exchange(): return lax.all_to_all(x, axis, 0, 0, tiled=True, axis_index_groups=groups)]
    all_to_all x3 -> x2, starting transfers between devices: 31 us -> 15.9 us  [_exchange(): return lax.all_to_all(x, axis, 0, 0, tiled=True, axis_index_groups=groups)]
    all_to_all x3 -> x2, waiting for transfers between devices: 10.2 us -> 1.91 us  [_exchange(): return lax.all_to_all(x, axis, 0, 0, tiled=True, axis_index_groups=groups)]
    ppermute x1, waiting for transfers between devices: 1.33 us -> 0.01 us  [local(): other_rows = lax.ppermute(query_rows, 'store', flip)]
    pallas_call x1, Pallas kernels: 1.14 us -> 0.4 us  [local(): pl.pallas_call(functools.partial(sketch_kernel, float(seq_len) ** (-0.5))...]
  transfers between devices with their start and end apart: 5 -> 4, of which waited for: 5 -> 2; matrix products, arithmetic and copies ran while one was open for 0% -> 0% of each run, Pallas kernels for 0% -> 0%
where the time goes in v5:
time: 57.2 us; the launch traced here: 56.8 us
  blocking collectives  24.7 us (43%)
  starting transfers between devices  20.4 us (36%)
  Pallas kernels  6.02 us (11%)
  waiting for transfers between devices  2.72 us (5%)
  local copies, waits for them, and re-layouts  1.98 us (3%)
  between operations  0.7 us (1%)
    all_to_all x1, blocking collectives, _exchange(): return lax.all_to_all(x, axis, 0, 0, tiled=True, axis_index_groups=groups)  24.7 us
    all_to_all x2, starting transfers between devices, _exchange(): return lax.all_to_all(x, axis, 0, 0, tiled=True, axis_index_groups=groups)  15.9 us
    pallas_call x1, Pallas kernels, local(): pl.pallas_call(functools.partial(factor_kernel, stores, step, store_order...  3.93 us
    ppermute x1, starting transfers between devices, local(): other_rows = lax.ppermute(query_rows, 'store', flip)  2.26 us
    ppermute x1, starting transfers between devices, local(): received = lax.ppermute(passed, 'store', flip)  2.25 us
    unnamed x8, local copies, waits for them, and re-layouts  1.98 us
    all_to_all x2, waiting for transfers between devices, _exchange(): return lax.all_to_all(x, axis, 0, 0, tiled=True, axis_index_groups=groups)  1.91 us
  transfers between devices with their start and end apart: 4, of which 2 were waited for; matrix products, arithmetic and copies ran while one was open for 0% of the time, Pallas kernels for 0%

profile of v5, /device:TPU:1, one launch (start us, length us, event | category | flops | bytes accessed | tf_op | source)
XLA Modules:
  0.0 56.8 jit_solution(12543972878352300681)
XLA Ops:
  0.6 3.9 %factors.1 = bf16[8,240,128]{2,1,0:T(8,128)(2,1)} custom-call(bf16[256,640]{1,0:T(8,128)(2,1)} %x_hbm.1, bf16[1728,256]{1,0:T(8,128)(2,1)} %bitcast.10, bf16[1728,256]{1,0:T(8,128)(2,1)} %bitcast.11, bf16[1728,256]{1,0:T(8,128)(2,1)} %bitcast.12, bf16[256,640]{1,0:T(8,128)(2,1)} %dy_hbm.1, bf16[640,128]{1,0:T(8,128)(2,1)} %pmi_hbm.1, ...), custom_call_target="tpu_custom_call" | custom-call | tf_op jit(solution)/shard_map/factors/pallas_call | solution.py:227
  4.6 0.0 copy-start
  4.6 10.9 %all-to-all-start = ((bf16[8,240,128]{2,1,0:T(8,128)(2,1)}), bf16[8,240,128]{2,1,0:T(8,128)(2,1)S(1)}, u32[]{:S(2)}, u32[]{:S(2)}) async-start(bf16[8,240,128]{2,1,0:T(8,128)(2,1)} %factors.1), calls=%async_computation | async-start | bytes 983040 | tf_op jit(solution)/shard_map/all_to_all | solution.py:26
  15.5 0.0 copy-done
  15.5 2.3 %collective-permute-start = (bf16[3,128,512]{2,1,0:T(8,128)(2,1)S(1)}, bf16[3,128,512]{2,1,0:T(8,128)(2,1)S(1)}, u32[]{:S(2)}, u32[]{:S(2)}) collective-permute-start(bf16[3,128,512]{2,1,0:T(8,128)(2,1)S(1)} %bitcast.8), channel_id=1, source_target_pairs={{0,1},{1,0},{2,3},{3,2},{4,5},{5,4},{6,7},{7,6},{8,9},{9,8},{10,11... | collective-permute-start | bytes 1179656 | tf_op jit(solution)/shard_map/ppermute | solution.py:282
  17.8 0.0 copy-start.1
  17.8 0.7 %copy-done.1 = s32[2,128]{1,0:T(2,128)S(1)} copy-done((s32[2,128]{1,0:T(2,128)S(1)}, s32[2,128]{1,0:T(2,128)}, u32[]{:S(2)}) %copy-start.1) | copy-done | bytes 1048
  18.4 0.0 copy-start.2
  18.4 0.6 %copy-done.2 = s32[128]{0:T(128)S(1)} copy-done((s32[128]{0:T(128)S(1)}, s32[128]{0:T(128)}, u32[]{:S(2)}) %copy-start.2) | copy-done | bytes 536
  19.1 0.0 copy-start.3
  19.1 0.6 %copy-done.3 = s32[64]{0:T(128)S(1)} copy-done((s32[64]{0:T(128)S(1)}, s32[64]{0:T(128)}, u32[]{:S(2)}) %copy-start.3) | copy-done | bytes 280
  19.8 0.1 select_reduce_fusion
  19.9 0.1 convolution_convert_fusion.chooser
  20.0 0.0 collective-permute-done.other
  20.0 1.9 %all-to-all-done.got = bf16[8,240,128]{2,1,0:T(8,128)(2,1)S(1)} async-done(((bf16[8,240,128]{2,1,0:T(8,128)(2,1)}), bf16[8,240,128]{2,1,0:T(8,128)(2,1)S(1)}, u32[]{:S(2)}, u32[]{:S(2)}) %all-to-all-start) | async-done | bytes 491552 | tf_op jit(solution)/shard_map/all_to_all | solution.py:26
  21.9 0.4 sketch.1
  22.3 24.7 %all_to_all.15.gathered = bf16[64,24,128]{2,1,0:T(8,128)(2,1)S(1)} all-to-all(bf16[64,24,128]{2,1,0:T(8,128)(2,1)S(1)} %sketch.1), channel_id=1, replica_groups={{288,0,400,472,184,416,280,224,424,256,8,240,368,216,72,80,104,480,232,..., dimensions={0} | all-to-all | bytes 786432 | tf_op jit(solution)/shard_map/all_to_all | solution.py:26
  47.0 1.1 %scores.1 = (f32[64,128]{1,0:T(8,128)}, bf16[3,4,512]{2,1,0:T(4,128)(2,1)S(1)}, bf16[3,4,512]{2,1,0:T(4,128)(2,1)S(1)}) custom-call(bf16[64,24,128]{2,1,0:T(8,128)(2,1)S(1)} %all_to_all.15.gathered, bf16[3,128,512]{2,1,0:T(8,128)(2,1)S(1)} %bitcast.9, bf16[3,128,512]{2,1,0:T(8,128)(2,1)S(1)} %collective-permute-done.other, ...), custom_call_target="tpu_custom_call" | custom-call | tf_op jit(solution)/shard_map/scores/pallas_call | solution.py:298
  48.1 5.0 %all-to-all-start.2 = ((f32[8,8,128]{2,1,0:T(8,128)}), f32[8,8,128]{2,1,0:T(8,128)S(1)}, u32[]{:S(2)}, u32[]{:S(2)}) async-start(f32[8,8,128]{2,1,0:T(8,128)} %bitcast.6), calls=%async_computation.2 | async-start | bytes 65536 | tf_op jit(solution)/shard_map/all_to_all | solution.py:26
  53.1 2.2 %collective-permute-start.1 = (bf16[3,4,512]{2,1,0:T(4,128)(2,1)S(1)}, bf16[3,4,512]{2,1,0:T(4,128)(2,1)S(1)}, u32[]{:S(2)}, u32[]{:S(2)}) collective-permute-start(bf16[3,4,512]{2,1,0:T(4,128)(2,1)S(1)} %get-tuple-element.9), channel_id=1, source_target_pairs={{0,1},{1,0},{2,3},{3,2},{4,5},{5,4},{6,7},{7,6},{8,9},{9,8},{10,11... | collective-permute-start | bytes 36872 | tf_op jit(solution)/shard_map/ppermute | solution.py:311
  55.4 0.8 %collective-permute-done.1.received = bf16[3,4,512]{2,1,0:T(4,128)(2,1)S(1)} collective-permute-done((bf16[3,4,512]{2,1,0:T(4,128)(2,1)S(1)}, bf16[3,4,512]{2,1,0:T(4,128)(2,1)S(1)}, u32[]{:S(2)}, u32[]{:S(2)}) %collective-permute-start.1) | collective-permute-done | bytes 12320 | tf_op jit(solution)/shard_map/ppermute | solution.py:311
  56.2 0.0 all-to-all-done.2.parts
  56.2 0.6 %finish.1 = (f32[16,128]{1,0:T(8,128)}, bf16[3,4,512]{2,1,0:T(4,128)(2,1)}) custom-call(f32[8,8,128]{2,1,0:T(8,128)S(1)} %all-to-all-done.2.parts, bf16[3,4,512]{2,1,0:T(4,128)(2,1)S(1)} %get-tuple-element.8.own, bf16[3,4,512]{2,1,0:T(4,128)(2,1)S(1)} %collective-permute-done.1.received), custom_call_target="tpu_custom_call" | custom-call | tf_op jit(solution)/shard_map/finish/pallas_call | solution.py:312
  (3 shorter events, 0.0 us)
Async XLA Ops:
  4.6 10.9 %copy-start = (bf16[128,3,512]{2,0,1:T(8,128)(2,1)S(1)}, bf16[128,3,512]{2,0,1:T(8,128)(2,1)}, u32[]{:S(2)}) copy-start(bf16[128,3,512]{2,0,1:T(8,128)(2,1)} %param.22) | copy-start | bytes 1179652
  4.6 17.3 %all-to-all-start = ((bf16[8,240,128]{2,1,0:T(8,128)(2,1)}), bf16[8,240,128]{2,1,0:T(8,128)(2,1)S(1)}, u32[]{:S(2)}, u32[]{:S(2)}) async-start(bf16[8,240,128]{2,1,0:T(8,128)(2,1)} %factors.1), calls=%async_computation | async-start | bytes 983040 | tf_op jit(solution)/shard_map/all_to_all | solution.py:26
  15.5 4.5 %collective-permute-start = (bf16[3,128,512]{2,1,0:T(8,128)(2,1)S(1)}, bf16[3,128,512]{2,1,0:T(8,128)(2,1)S(1)}, u32[]{:S(2)}, u32[]{:S(2)}) collective-permute-start(bf16[3,128,512]{2,1,0:T(8,128)(2,1)S(1)} %bitcast.8), channel_id=1, source_target_pairs={{0,1},{1,0},{2,3},{3,2},{4,5},{5,4},{6,7},{7,6},{8,9},{9,8},{10,11... | collective-permute-start | bytes 1179656 | tf_op jit(solution)/shard_map/ppermute | solution.py:282
  17.8 0.7 %copy-start.1 = (s32[2,128]{1,0:T(2,128)S(1)}, s32[2,128]{1,0:T(2,128)}, u32[]{:S(2)}) copy-start(s32[2,128]{1,0:T(2,128)} %param.23) | copy-start | bytes 3076
  18.4 0.7 %copy-start.2 = (s32[128]{0:T(128)S(1)}, s32[128]{0:T(128)}, u32[]{:S(2)}) copy-start(s32[128]{0:T(128)} %param.24) | copy-start | bytes 1540
  19.1 0.7 %copy-start.3 = (s32[64]{0:T(128)S(1)}, s32[64]{0:T(128)}, u32[]{:S(2)}) copy-start(s32[64]{0:T(128)} %constant.26.clone) | copy-start | bytes 772
  48.1 8.2 %all-to-all-start.2 = ((f32[8,8,128]{2,1,0:T(8,128)}), f32[8,8,128]{2,1,0:T(8,128)S(1)}, u32[]{:S(2)}, u32[]{:S(2)}) async-start(f32[8,8,128]{2,1,0:T(8,128)} %bitcast.6), calls=%async_computation.2 | async-start | bytes 65536 | tf_op jit(solution)/shard_map/all_to_all | solution.py:26
  53.1 3.1 %collective-permute-start.1 = (bf16[3,4,512]{2,1,0:T(4,128)(2,1)S(1)}, bf16[3,4,512]{2,1,0:T(4,128)(2,1)S(1)}, u32[]{:S(2)}, u32[]{:S(2)}) collective-permute-start(bf16[3,4,512]{2,1,0:T(4,128)(2,1)S(1)} %get-tuple-element.9), channel_id=1, source_target_pairs={{0,1},{1,0},{2,3},{3,2},{4,5},{5,4},{6,7},{7,6},{8,9},{9,8},{10,11... | collective-permute-start | bytes 36872 | tf_op jit(solution)/shard_map/ppermute | solution.py:311

commit v6 on v5

--- a/solution.py
+++ b/solution.py
@@ -10,7 +10,7 @@
 
 BF = jnp.bfloat16
 F32 = jnp.float32
-GROUP_SEED = 2
+GROUP_SEED = 29
 STORE_SEED = 8
 
 

time: 57.2 us -> 56.9 us (level)
  blocking collectives: 24.7 us -> 24 us
    all_to_all x1, blocking collectives: 24.7 us -> 24 us  [_exchange(): return lax.all_to_all(x, axis, 0, 0, tiled=True, axis_index_groups=groups)]
  transfers between devices with their start and end apart: 4 -> 4, of which waited for: 2 -> 3; matrix products, arithmetic and copies ran while one was open for 0% -> 0% of each run, Pallas kernels for 0% -> 0%
where the time goes in v6:
time: 56.9 us; the launch traced here: 56.5 us
  blocking collectives  24 us (42%)
  starting transfers between devices  20.6 us (36%)
  Pallas kernels  6.03 us (11%)
  waiting for transfers between devices  2.95 us (5%)
  local copies, waits for them, and re-layouts  1.98 us (3%)
  between operations  0.7 us (1%)
    all_to_all x1, blocking collectives, _exchange(): return lax.all_to_all(x, axis, 0, 0, tiled=True, axis_index_groups=groups)  24 us
    all_to_all x2, starting transfers between devices, _exchange(): return lax.all_to_all(x, axis, 0, 0, tiled=True, axis_index_groups=groups)  16.1 us
    pallas_call x1, Pallas kernels, local(): pl.pallas_call(functools.partial(factor_kernel, stores, step, store_order...  3.93 us
    ppermute x1, starting transfers between devices, local(): other_rows = lax.ppermute(query_rows, 'store', flip)  2.26 us
    ppermute x1, starting transfers between devices, local(): received = lax.ppermute(passed, 'store', flip)  2.26 us
    all_to_all x2, waiting for transfers between devices, _exchange(): return lax.all_to_all(x, axis, 0, 0, tiled=True, axis_index_groups=groups)  2.14 us
    unnamed x8, local copies, waits for them, and re-layouts  1.98 us
  transfers between devices with their start and end apart: 4, of which 3 were waited for; matrix products, arithmetic and copies ran while one was open for 0% of the time, Pallas kernels for 0%

profile of v6, /device:TPU:1, one launch (start us, length us, event | category | flops | bytes accessed | tf_op | source)
XLA Modules:
  0.0 56.5 jit_solution(11035290365823177761)
XLA Ops:
  0.6 3.9 %factors.1 = bf16[8,240,128]{2,1,0:T(8,128)(2,1)} custom-call(bf16[256,640]{1,0:T(8,128)(2,1)} %x_hbm.1, bf16[1728,256]{1,0:T(8,128)(2,1)} %bitcast.10, bf16[1728,256]{1,0:T(8,128)(2,1)} %bitcast.11, bf16[1728,256]{1,0:T(8,128)(2,1)} %bitcast.12, bf16[256,640]{1,0:T(8,128)(2,1)} %dy_hbm.1, bf16[640,128]{1,0:T(8,128)(2,1)} %pmi_hbm.1, ...), custom_call_target="tpu_custom_call" | custom-call | tf_op jit(solution)/shard_map/factors/pallas_call | solution.py:227
  4.6 0.0 copy-start
  4.6 10.9 %all-to-all-start = ((bf16[8,240,128]{2,1,0:T(8,128)(2,1)}), bf16[8,240,128]{2,1,0:T(8,128)(2,1)S(1)}, u32[]{:S(2)}, u32[]{:S(2)}) async-start(bf16[8,240,128]{2,1,0:T(8,128)(2,1)} %factors.1), calls=%async_computation | async-start | bytes 983040 | tf_op jit(solution)/shard_map/all_to_all | solution.py:26
  15.5 0.0 copy-done
  15.5 2.3 %collective-permute-start = (bf16[3,128,512]{2,1,0:T(8,128)(2,1)S(1)}, bf16[3,128,512]{2,1,0:T(8,128)(2,1)S(1)}, u32[]{:S(2)}, u32[]{:S(2)}) collective-permute-start(bf16[3,128,512]{2,1,0:T(8,128)(2,1)S(1)} %bitcast.8), channel_id=1, source_target_pairs={{0,1},{1,0},{2,3},{3,2},{4,5},{5,4},{6,7},{7,6},{8,9},{9,8},{10,11... | collective-permute-start | bytes 1179656 | tf_op jit(solution)/shard_map/ppermute | solution.py:282
  17.8 0.0 copy-start.1
  17.8 0.7 %copy-done.1 = s32[2,128]{1,0:T(2,128)S(1)} copy-done((s32[2,128]{1,0:T(2,128)S(1)}, s32[2,128]{1,0:T(2,128)}, u32[]{:S(2)}) %copy-start.1) | copy-done | bytes 1048
  18.4 0.0 copy-start.2
  18.4 0.6 %copy-done.2 = s32[128]{0:T(128)S(1)} copy-done((s32[128]{0:T(128)S(1)}, s32[128]{0:T(128)}, u32[]{:S(2)}) %copy-start.2) | copy-done | bytes 536
  19.1 0.0 copy-start.3
  19.1 0.6 %copy-done.3 = s32[64]{0:T(128)S(1)} copy-done((s32[64]{0:T(128)S(1)}, s32[64]{0:T(128)}, u32[]{:S(2)}) %copy-start.3) | copy-done | bytes 280
  19.8 0.1 select_reduce_fusion
  19.9 0.1 convolution_convert_fusion.chooser
  20.0 0.0 collective-permute-done.other
  20.0 1.9 %all-to-all-done.got = bf16[8,240,128]{2,1,0:T(8,128)(2,1)S(1)} async-done(((bf16[8,240,128]{2,1,0:T(8,128)(2,1)}), bf16[8,240,128]{2,1,0:T(8,128)(2,1)S(1)}, u32[]{:S(2)}, u32[]{:S(2)}) %all-to-all-start) | async-done | bytes 491552 | tf_op jit(solution)/shard_map/all_to_all | solution.py:26
  21.9 0.4 sketch.1
  22.3 24.0 %all_to_all.15.gathered = bf16[64,24,128]{2,1,0:T(8,128)(2,1)S(1)} all-to-all(bf16[64,24,128]{2,1,0:T(8,128)(2,1)S(1)} %sketch.1), channel_id=1, replica_groups={{368,312,136,56,200,72,280,80,432,416,232,224,48,32,424,480,8,64,472,12..., dimensions={0} | all-to-all | bytes 786432 | tf_op jit(solution)/shard_map/all_to_all | solution.py:26
  46.3 1.1 %scores.1 = (f32[64,128]{1,0:T(8,128)}, bf16[3,4,512]{2,1,0:T(4,128)(2,1)S(1)}, bf16[3,4,512]{2,1,0:T(4,128)(2,1)S(1)}) custom-call(bf16[64,24,128]{2,1,0:T(8,128)(2,1)S(1)} %all_to_all.15.gathered, bf16[3,128,512]{2,1,0:T(8,128)(2,1)S(1)} %bitcast.9, bf16[3,128,512]{2,1,0:T(8,128)(2,1)S(1)} %collective-permute-done.other, ...), custom_call_target="tpu_custom_call" | custom-call | tf_op jit(solution)/shard_map/scores/pallas_call | solution.py:298
  47.4 5.2 %all-to-all-start.2 = ((f32[8,8,128]{2,1,0:T(8,128)}), f32[8,8,128]{2,1,0:T(8,128)S(1)}, u32[]{:S(2)}, u32[]{:S(2)}) async-start(f32[8,8,128]{2,1,0:T(8,128)} %bitcast.6), calls=%async_computation.2 | async-start | bytes 65536 | tf_op jit(solution)/shard_map/all_to_all | solution.py:26
  52.5 2.3 %collective-permute-start.1 = (bf16[3,4,512]{2,1,0:T(4,128)(2,1)S(1)}, bf16[3,4,512]{2,1,0:T(4,128)(2,1)S(1)}, u32[]{:S(2)}, u32[]{:S(2)}) collective-permute-start(bf16[3,4,512]{2,1,0:T(4,128)(2,1)S(1)} %get-tuple-element.9), channel_id=1, source_target_pairs={{0,1},{1,0},{2,3},{3,2},{4,5},{5,4},{6,7},{7,6},{8,9},{9,8},{10,11... | collective-permute-start | bytes 36872 | tf_op jit(solution)/shard_map/ppermute | solution.py:311
  54.8 0.8 %collective-permute-done.1.received = bf16[3,4,512]{2,1,0:T(4,128)(2,1)S(1)} collective-permute-done((bf16[3,4,512]{2,1,0:T(4,128)(2,1)S(1)}, bf16[3,4,512]{2,1,0:T(4,128)(2,1)S(1)}, u32[]{:S(2)}, u32[]{:S(2)}) %collective-permute-start.1) | collective-permute-done | bytes 12320 | tf_op jit(solution)/shard_map/ppermute | solution.py:311
  55.6 0.3 all-to-all-done.2.parts
  55.9 0.6 %finish.1 = (f32[16,128]{1,0:T(8,128)}, bf16[3,4,512]{2,1,0:T(4,128)(2,1)}) custom-call(f32[8,8,128]{2,1,0:T(8,128)S(1)} %all-to-all-done.2.parts, bf16[3,4,512]{2,1,0:T(4,128)(2,1)S(1)} %get-tuple-element.8.own, bf16[3,4,512]{2,1,0:T(4,128)(2,1)S(1)} %collective-permute-done.1.received), custom_call_target="tpu_custom_call" | custom-call | tf_op jit(solution)/shard_map/finish/pallas_call | solution.py:312
  (3 shorter events, 0.0 us)
Async XLA Ops:
  4.6 10.9 %copy-start = (bf16[128,3,512]{2,0,1:T(8,128)(2,1)S(1)}, bf16[128,3,512]{2,0,1:T(8,128)(2,1)}, u32[]{:S(2)}) copy-start(bf16[128,3,512]{2,0,1:T(8,128)(2,1)} %param.22) | copy-start | bytes 1179652
  4.6 17.3 %all-to-all-start = ((bf16[8,240,128]{2,1,0:T(8,128)(2,1)}), bf16[8,240,128]{2,1,0:T(8,128)(2,1)S(1)}, u32[]{:S(2)}, u32[]{:S(2)}) async-start(bf16[8,240,128]{2,1,0:T(8,128)(2,1)} %factors.1), calls=%async_computation | async-start | bytes 983040 | tf_op jit(solution)/shard_map/all_to_all | solution.py:26
  15.5 4.5 %collective-permute-start = (bf16[3,128,512]{2,1,0:T(8,128)(2,1)S(1)}, bf16[3,128,512]{2,1,0:T(8,128)(2,1)S(1)}, u32[]{:S(2)}, u32[]{:S(2)}) collective-permute-start(bf16[3,128,512]{2,1,0:T(8,128)(2,1)S(1)} %bitcast.8), channel_id=1, source_target_pairs={{0,1},{1,0},{2,3},{3,2},{4,5},{5,4},{6,7},{7,6},{8,9},{9,8},{10,11... | collective-permute-start | bytes 1179656 | tf_op jit(solution)/shard_map/ppermute | solution.py:282
  17.8 0.7 %copy-start.1 = (s32[2,128]{1,0:T(2,128)S(1)}, s32[2,128]{1,0:T(2,128)}, u32[]{:S(2)}) copy-start(s32[2,128]{1,0:T(2,128)} %param.23) | copy-start | bytes 3076
  18.4 0.7 %copy-start.2 = (s32[128]{0:T(128)S(1)}, s32[128]{0:T(128)}, u32[]{:S(2)}) copy-start(s32[128]{0:T(128)} %param.24) | copy-start | bytes 1540
  19.1 0.7 %copy-start.3 = (s32[64]{0:T(128)S(1)}, s32[64]{0:T(128)}, u32[]{:S(2)}) copy-start(s32[64]{0:T(128)} %constant.26.clone) | copy-start | bytes 772
  47.4 8.5 %all-to-all-start.2 = ((f32[8,8,128]{2,1,0:T(8,128)}), f32[8,8,128]{2,1,0:T(8,128)S(1)}, u32[]{:S(2)}, u32[]{:S(2)}) async-start(f32[8,8,128]{2,1,0:T(8,128)} %bitcast.6), calls=%async_computation.2 | async-start | bytes 65536 | tf_op jit(solution)/shard_map/all_to_all | solution.py:26
  52.5 3.1 %collective-permute-start.1 = (bf16[3,4,512]{2,1,0:T(4,128)(2,1)S(1)}, bf16[3,4,512]{2,1,0:T(4,128)(2,1)S(1)}, u32[]{:S(2)}, u32[]{:S(2)}) collective-permute-start(bf16[3,4,512]{2,1,0:T(4,128)(2,1)S(1)} %get-tuple-element.9), channel_id=1, source_target_pairs={{0,1},{1,0},{2,3},{3,2},{4,5},{5,4},{6,7},{7,6},{8,9},{9,8},{10,11... | collective-permute-start | bytes 36872 | tf_op jit(solution)/shard_map/ppermute | solution.py:311

commit v7 on v6

--- a/solution.py
+++ b/solution.py
@@ -11,7 +11,7 @@
 BF = jnp.bfloat16
 F32 = jnp.float32
 GROUP_SEED = 29
-STORE_SEED = 8
+STORE_SEED = 9
 
 
 def _order(count, seed):

time: 56.9 us -> 57.1 us (level)
  transfers between devices with their start and end apart: 4 -> 4, of which waited for: 3 -> 2; matrix products, arithmetic and copies ran while one was open for 0% -> 0% of each run, Pallas kernels for 0% -> 0%
where the time goes in v7:
time: 57.1 us; the launch traced here: 56.7 us
  blocking collectives  24 us (42%)
  starting transfers between devices  20.4 us (36%)
  Pallas kernels  6.03 us (11%)
  waiting for transfers between devices  3.28 us (6%)
  local copies, waits for them, and re-layouts  1.98 us (3%)
  between operations  0.7 us (1%)
    all_to_all x1, blocking collectives, _exchange(): return lax.all_to_all(x, axis, 0, 0, tiled=True, axis_index_groups=groups)  24 us
    all_to_all x2, starting transfers between devices, _exchange(): return lax.all_to_all(x, axis, 0, 0, tiled=True, axis_index_groups=groups)  15.8 us
    pallas_call x1, Pallas kernels, local(): pl.pallas_call(functools.partial(factor_kernel, stores, step, store_order...  3.93 us
    all_to_all x2, waiting for transfers between devices, _exchange(): return lax.all_to_all(x, axis, 0, 0, tiled=True, axis_index_groups=groups)  2.47 us
    ppermute x1, starting transfers between devices, local(): other_rows = lax.ppermute(query_rows, 'store', flip)  2.33 us
    ppermute x1, starting transfers between devices, local(): received = lax.ppermute(passed, 'store', flip)  2.32 us
    unnamed x8, local copies, waits for them, and re-layouts  1.98 us
  transfers between devices with their start and end apart: 4, of which 2 were waited for; matrix products, arithmetic and copies ran while one was open for 0% of the time, Pallas kernels for 0%

profile of v7, /device:TPU:1, one launch (start us, length us, event | category | flops | bytes accessed | tf_op | source)
XLA Modules:
  0.0 56.7 jit_solution(1303036464121546026)
XLA Ops:
  0.6 3.9 %factors.1 = bf16[8,240,128]{2,1,0:T(8,128)(2,1)} custom-call(bf16[256,640]{1,0:T(8,128)(2,1)} %x_hbm.1, bf16[1728,256]{1,0:T(8,128)(2,1)} %bitcast.10, bf16[1728,256]{1,0:T(8,128)(2,1)} %bitcast.11, bf16[1728,256]{1,0:T(8,128)(2,1)} %bitcast.12, bf16[256,640]{1,0:T(8,128)(2,1)} %dy_hbm.1, bf16[640,128]{1,0:T(8,128)(2,1)} %pmi_hbm.1, ...), custom_call_target="tpu_custom_call" | custom-call | tf_op jit(solution)/shard_map/factors/pallas_call | solution.py:227
  4.6 0.0 copy-start
  4.6 10.9 %all-to-all-start = ((bf16[8,240,128]{2,1,0:T(8,128)(2,1)}), bf16[8,240,128]{2,1,0:T(8,128)(2,1)S(1)}, u32[]{:S(2)}, u32[]{:S(2)}) async-start(bf16[8,240,128]{2,1,0:T(8,128)(2,1)} %factors.1), calls=%async_computation | async-start | bytes 983040 | tf_op jit(solution)/shard_map/all_to_all | solution.py:26
  15.4 0.0 copy-done
  15.4 2.3 %collective-permute-start = (bf16[3,128,512]{2,1,0:T(8,128)(2,1)S(1)}, bf16[3,128,512]{2,1,0:T(8,128)(2,1)S(1)}, u32[]{:S(2)}, u32[]{:S(2)}) collective-permute-start(bf16[3,128,512]{2,1,0:T(8,128)(2,1)S(1)} %bitcast.8), channel_id=1, source_target_pairs={{0,1},{1,0},{2,3},{3,2},{4,5},{5,4},{6,7},{7,6},{8,9},{9,8},{10,11... | collective-permute-start | bytes 1179656 | tf_op jit(solution)/shard_map/ppermute | solution.py:282
  17.8 0.0 copy-start.1
  17.8 0.7 %copy-done.1 = s32[2,128]{1,0:T(2,128)S(1)} copy-done((s32[2,128]{1,0:T(2,128)S(1)}, s32[2,128]{1,0:T(2,128)}, u32[]{:S(2)}) %copy-start.1) | copy-done | bytes 1048
  18.5 0.0 copy-start.2
  18.5 0.6 %copy-done.2 = s32[128]{0:T(128)S(1)} copy-done((s32[128]{0:T(128)S(1)}, s32[128]{0:T(128)}, u32[]{:S(2)}) %copy-start.2) | copy-done | bytes 536
  19.1 0.0 copy-start.3
  19.1 0.6 %copy-done.3 = s32[64]{0:T(128)S(1)} copy-done((s32[64]{0:T(128)S(1)}, s32[64]{0:T(128)}, u32[]{:S(2)}) %copy-start.3) | copy-done | bytes 280
  19.8 0.1 select_reduce_fusion
  19.9 0.1 convolution_convert_fusion.chooser
  20.0 0.0 collective-permute-done.other
  20.0 2.5 %all-to-all-done.got = bf16[8,240,128]{2,1,0:T(8,128)(2,1)S(1)} async-done(((bf16[8,240,128]{2,1,0:T(8,128)(2,1)}), bf16[8,240,128]{2,1,0:T(8,128)(2,1)S(1)}, u32[]{:S(2)}, u32[]{:S(2)}) %all-to-all-start) | async-done | bytes 491552 | tf_op jit(solution)/shard_map/all_to_all | solution.py:26
  22.5 0.4 sketch.1
  22.9 24.0 %all_to_all.15.gathered = bf16[64,24,128]{2,1,0:T(8,128)(2,1)S(1)} all-to-all(bf16[64,24,128]{2,1,0:T(8,128)(2,1)S(1)} %sketch.1), channel_id=1, replica_groups={{368,312,136,56,200,72,280,80,432,416,232,224,48,32,424,480,8,64,472,12..., dimensions={0} | all-to-all | bytes 786432 | tf_op jit(solution)/shard_map/all_to_all | solution.py:26
  46.9 1.1 %scores.1 = (f32[64,128]{1,0:T(8,128)}, bf16[3,4,512]{2,1,0:T(4,128)(2,1)S(1)}, bf16[3,4,512]{2,1,0:T(4,128)(2,1)S(1)}) custom-call(bf16[64,24,128]{2,1,0:T(8,128)(2,1)S(1)} %all_to_all.15.gathered, bf16[3,128,512]{2,1,0:T(8,128)(2,1)S(1)} %bitcast.9, bf16[3,128,512]{2,1,0:T(8,128)(2,1)S(1)} %collective-permute-done.other, ...), custom_call_target="tpu_custom_call" | custom-call | tf_op jit(solution)/shard_map/scores/pallas_call | solution.py:298
  48.0 4.9 %all-to-all-start.2 = ((f32[8,8,128]{2,1,0:T(8,128)}), f32[8,8,128]{2,1,0:T(8,128)S(1)}, u32[]{:S(2)}, u32[]{:S(2)}) async-start(f32[8,8,128]{2,1,0:T(8,128)} %bitcast.6), calls=%async_computation.2 | async-start | bytes 65536 | tf_op jit(solution)/shard_map/all_to_all | solution.py:26
  52.9 2.3 %collective-permute-start.1 = (bf16[3,4,512]{2,1,0:T(4,128)(2,1)S(1)}, bf16[3,4,512]{2,1,0:T(4,128)(2,1)S(1)}, u32[]{:S(2)}, u32[]{:S(2)}) collective-permute-start(bf16[3,4,512]{2,1,0:T(4,128)(2,1)S(1)} %get-tuple-element.9), channel_id=1, source_target_pairs={{0,1},{1,0},{2,3},{3,2},{4,5},{5,4},{6,7},{7,6},{8,9},{9,8},{10,11... | collective-permute-start | bytes 36872 | tf_op jit(solution)/shard_map/ppermute | solution.py:311
  55.2 0.8 %collective-permute-done.1.received = bf16[3,4,512]{2,1,0:T(4,128)(2,1)S(1)} collective-permute-done((bf16[3,4,512]{2,1,0:T(4,128)(2,1)S(1)}, bf16[3,4,512]{2,1,0:T(4,128)(2,1)S(1)}, u32[]{:S(2)}, u32[]{:S(2)}) %collective-permute-start.1) | collective-permute-done | bytes 12320 | tf_op jit(solution)/shard_map/ppermute | solution.py:311
  56.0 0.0 all-to-all-done.2.parts
  56.0 0.6 %finish.1 = (f32[16,128]{1,0:T(8,128)}, bf16[3,4,512]{2,1,0:T(4,128)(2,1)}) custom-call(f32[8,8,128]{2,1,0:T(8,128)S(1)} %all-to-all-done.2.parts, bf16[3,4,512]{2,1,0:T(4,128)(2,1)S(1)} %get-tuple-element.8.own, bf16[3,4,512]{2,1,0:T(4,128)(2,1)S(1)} %collective-permute-done.1.received), custom_call_target="tpu_custom_call" | custom-call | tf_op jit(solution)/shard_map/finish/pallas_call | solution.py:312
  (3 shorter events, 0.0 us)
Async XLA Ops:
  4.6 10.9 %copy-start = (bf16[128,3,512]{2,0,1:T(8,128)(2,1)S(1)}, bf16[128,3,512]{2,0,1:T(8,128)(2,1)}, u32[]{:S(2)}) copy-start(bf16[128,3,512]{2,0,1:T(8,128)(2,1)} %param.22) | copy-start | bytes 1179652
  4.6 17.9 %all-to-all-start = ((bf16[8,240,128]{2,1,0:T(8,128)(2,1)}), bf16[8,240,128]{2,1,0:T(8,128)(2,1)S(1)}, u32[]{:S(2)}, u32[]{:S(2)}) async-start(bf16[8,240,128]{2,1,0:T(8,128)(2,1)} %factors.1), calls=%async_computation | async-start | bytes 983040 | tf_op jit(solution)/shard_map/all_to_all | solution.py:26
  15.4 4.6 %collective-permute-start = (bf16[3,128,512]{2,1,0:T(8,128)(2,1)S(1)}, bf16[3,128,512]{2,1,0:T(8,128)(2,1)S(1)}, u32[]{:S(2)}, u32[]{:S(2)}) collective-permute-start(bf16[3,128,512]{2,1,0:T(8,128)(2,1)S(1)} %bitcast.8), channel_id=1, source_target_pairs={{0,1},{1,0},{2,3},{3,2},{4,5},{5,4},{6,7},{7,6},{8,9},{9,8},{10,11... | collective-permute-start | bytes 1179656 | tf_op jit(solution)/shard_map/ppermute | solution.py:282
  17.8 0.7 %copy-start.1 = (s32[2,128]{1,0:T(2,128)S(1)}, s32[2,128]{1,0:T(2,128)}, u32[]{:S(2)}) copy-start(s32[2,128]{1,0:T(2,128)} %param.23) | copy-start | bytes 3076
  18.5 0.7 %copy-start.2 = (s32[128]{0:T(128)S(1)}, s32[128]{0:T(128)}, u32[]{:S(2)}) copy-start(s32[128]{0:T(128)} %param.24) | copy-start | bytes 1540
  19.1 0.7 %copy-start.3 = (s32[64]{0:T(128)S(1)}, s32[64]{0:T(128)}, u32[]{:S(2)}) copy-start(s32[64]{0:T(128)} %constant.26.clone) | copy-start | bytes 772
  48.0 8.1 %all-to-all-start.2 = ((f32[8,8,128]{2,1,0:T(8,128)}), f32[8,8,128]{2,1,0:T(8,128)S(1)}, u32[]{:S(2)}, u32[]{:S(2)}) async-start(f32[8,8,128]{2,1,0:T(8,128)} %bitcast.6), calls=%async_computation.2 | async-start | bytes 65536 | tf_op jit(solution)/shard_map/all_to_all | solution.py:26
  52.9 3.1 %collective-permute-start.1 = (bf16[3,4,512]{2,1,0:T(4,128)(2,1)S(1)}, bf16[3,4,512]{2,1,0:T(4,128)(2,1)S(1)}, u32[]{:S(2)}, u32[]{:S(2)}) collective-permute-start(bf16[3,4,512]{2,1,0:T(4,128)(2,1)S(1)} %get-tuple-element.9), channel_id=1, source_target_pairs={{0,1},{1,0},{2,3},{3,2},{4,5},{5,4},{6,7},{7,6},{8,9},{9,8},{10,11... | collective-permute-start | bytes 36872 | tf_op jit(solution)/shard_map/ppermute | solution.py:311
